TPU v7x, 32 devices: a whole 2x2x4 slice. The times are simulated.
32 devices in a mesh: dp: 16 (over z, x, core), fsdp: 2 (over y).
Axes of the slice: x: 2, y: 2, z: 4, core: 2. Of those that a mesh axis runs over, the one named last changes fastest.
Arguments:
- tokens: bfloat16 [4096, 768], P(('dp', 'fsdp')), may hold values from -6 to 6
- query_weight: bfloat16 [768, 768], P(('dp', 'fsdp')), may hold values from -0.21875 to 0.21875
- key_weight: bfloat16 [768, 768], P(('dp', 'fsdp')), may hold values from -0.21875 to 0.21875
- value_weight: bfloat16 [768, 768], P(('dp', 'fsdp')), may hold values from -0.21875 to 0.21875
- query_bias: bfloat16 [768], P(('dp', 'fsdp')), may hold values from -3 to 3
- value_bias: bfloat16 [768], P(('dp', 'fsdp')), may hold values from -3 to 3
- out_weight: bfloat16 [768, 768], P(('dp', 'fsdp')), may hold values from -1.75 to 1.75
- out_bias: bfloat16 [768], P(('dp', 'fsdp')), may hold values from -3 to 3
- first_gain: bfloat16 [768], P(('dp', 'fsdp')), may hold values from 0.25 to 1.75
- first_shift: bfloat16 [768], P(('dp', 'fsdp')), may hold values from -3 to 3
- up_weight: bfloat16 [768, 3072], P(('dp', 'fsdp')), may hold values from -0.21875 to 0.21875
- up_bias: bfloat16 [3072], P(('dp', 'fsdp')), may hold values from -3 to 3
- down_weight: bfloat16 [3072, 768], P(('dp', 'fsdp')), may hold values from -0.109375 to 0.109375
- down_bias: bfloat16 [768], P(('dp', 'fsdp')), may hold values from -3 to 3
- second_gain: bfloat16 [768], P(('dp', 'fsdp')), may hold values from 0.25 to 1.75
- second_shift: bfloat16 [768], P(('dp', 'fsdp')), may hold values from -3 to 3
- segment_ids: int32 [32, 128], P(('dp', 'fsdp')), may hold values from 0 to 2, never falling along the last dimension, each value on 1 to 96 neighbouring positions
- out_grad: bfloat16 [4096, 768], P(('dp', 'fsdp')), may hold values from -12 to 12
Outputs:
- layer_output: bfloat16 [4096, 768], P(('dp', 'fsdp'))
- input_grad: float32 [4096, 768], P(('dp', 'fsdp'))
- grad_query_weight: float32 [768, 768], P(('dp', 'fsdp'))
- grad_key_weight: float32 [768, 768], P(('dp', 'fsdp'))
- grad_value_weight: float32 [768, 768], P(('dp', 'fsdp'))
- grad_query_bias: float32 [768], P(('dp', 'fsdp'))
- grad_value_bias: float32 [768], P(('dp', 'fsdp'))
- grad_out_weight: float32 [768, 768], P(('dp', 'fsdp'))
- grad_out_bias: float32 [768], P(('dp', 'fsdp'))
- grad_first_gain: float32 [768], P(('dp', 'fsdp'))
- grad_first_shift: float32 [768], P(('dp', 'fsdp'))
- grad_up_weight: float32 [768, 3072], P(('dp', 'fsdp'))
- grad_up_bias: float32 [3072], P(('dp', 'fsdp'))
- grad_down_weight: float32 [3072, 768], P(('dp', 'fsdp'))
- grad_down_bias: float32 [768], P(('dp', 'fsdp'))
- grad_second_gain: float32 [768], P(('dp', 'fsdp'))
- grad_second_shift: float32 [768], P(('dp', 'fsdp'))
Inputs may be any that keep to these rules, and one draw needn't show every extreme that they name: `segment_ids`: numbers never fall along a sequence; each document holds at most 96 tokens.
All inputs are finite; a program needn't handle non-finite values.
Results may differ from a plain program's by a relative error of at most 0.015.
Values may be sent and summed in bfloat16 or wider, within the bound.
A program may use at most 128 MiB of HBM per device.

v0:
```python
from functools import partial

import jax
import jax.numpy as jnp
from jax import lax
from jax.experimental import pallas as pl
from jax.experimental.pallas import tpu as pltpu
from jax.sharding import PartitionSpec as P

HD = 64
MESH = pl.DeviceIdType.MESH
TILE = 16


def dims_of(dp, fsdp):
    core = (fsdp, 2 if dp % 2 == 0 else 1)
    rest, stride = dp // core[1], fsdp * core[1]
    sizes = []
    while rest > 1:
        step = 2 if rest % 4 else 4
        if not sizes and rest % 2 == 0:
            step = 2
        if rest % step:
            step = rest
        sizes.append((stride, step))
        stride, rest = stride * step, rest // step
    return core, [(1, fsdp)] + sizes


def plan_of(dp, fsdp, rows):
    core, links = dims_of(dp, fsdp)
    tiles = rows // TILE
    if len(links) != 3 or tiles < 3:
        return [(0, rows, [core] + links)]
    y, x, z = links
    outer = max(1, (tiles * 3 + 4) // 8)
    inner = tiles - 2 * outer
    orders = [[core, y, x, z], [core, z, y, x], [core, x, z, y]]
    plan, start = [], 0
    for count, order in zip((outer, inner, outer), orders):
        plan.append((start * TILE, count * TILE, order))
        start += count
    return plan


def prod_of(order):
    total = 1
    for _, size in order:
        total *= size
    return total


def coord(me, dim):
    return lax.rem(me // dim[0], dim[1])


def moved(slab, dim, old, new):
    return slab + (new - old) * dim[0]


def spread(slab, me, dims, k):
    for dim in reversed(dims):
        slab = moved(slab, dim, coord(me, dim), lax.rem(k, dim[1]))
        k = k // dim[1]
    return slab


def whoami(fsdp):
    return lax.axis_index("dp") * fsdp + lax.axis_index("fsdp")


def place(number, fsdp):
    return (number // fsdp, lax.rem(number, fsdp))


def greet(me, dims, fsdp):
    barrier = pltpu.get_barrier_semaphore()
    count = 0
    for dim in dims:
        mine = coord(me, dim)
        for r in range(dim[1] - 1):
            peer = moved(me, dim, mine, lax.rem(mine + 1 + r, dim[1]))
            pl.semaphore_signal(barrier, inc=1, device_id=place(peer, fsdp), device_id_type=MESH)
            count += 1
    pl.semaphore_wait(barrier, count)


def gather_kernel(dp, fsdp, plan, x_ref, out_ref, send_sem, recv_sem, own_sem):
    me = whoami(fsdp)
    greet(me, plan[0][2], fsdp)
    own = pltpu.make_async_copy(x_ref, out_ref.at[me], own_sem)
    own.start()

    def copy_of(band, slab, slot, peer, first):
        start, rows, _ = plan[band]
        here = out_ref.at[slab, pl.ds(start, rows), :]
        source = x_ref.at[pl.ds(start, rows), :] if first else here
        return pltpu.make_async_remote_copy(
            src_ref=source,
            dst_ref=here,
            send_sem=send_sem.at[band, slot],
            recv_sem=recv_sem.at[band, slab],
            device_id=place(peer, fsdp),
            device_id_type=MESH,
        )

    bases = []
    for _, _, order in plan:
        tree = order[1:] + order[:1]
        base, at = {}, 0
        for i in range(-1, len(tree)):
            arrivals = 1 if i < 0 else prod_of(tree[:i]) * (tree[i][1] - 1)
            for j in range(i + 1, len(tree)):
                base[i, j] = at
                at += arrivals * (tree[j][1] - 1)
        bases.append(base)
    depth = len(plan[0][2])
    for i in range(-1, depth):
        for band in range(len(plan)):
            order = plan[band][2]
            tree = order[1:] + order[:1]

            def sends(slab, k, act, i=i, band=band, tree=tree):
                for j in range(i + 1, depth):
                    dim = tree[j]
                    mine = coord(me, dim)
                    for r in range(dim[1] - 1):
                        peer = moved(me, dim, mine, lax.rem(mine + 1 + r, dim[1]))
                        slot = bases[band][i, j] + k * (dim[1] - 1) + r
                        act(copy_of(band, slab, slot, peer, i < 0))

            if i < 0:
                sends(me, 0, lambda c: c.start())
                continue
            dim = tree[i]
            mine = coord(me, dim)

            def arrived(k, _, i=i, band=band, tree=tree, dim=dim, mine=mine, sends=sends):
                gap = dim[1] - 1
                peer = moved(me, dim, mine, lax.rem(mine + 1 + lax.rem(k, gap), dim[1]))
                slab = spread(peer, me, tree[:i], k // gap)
                copy_of(band, slab, 0, peer, False).wait_recv()
                sends(slab, k, lambda c: c.start())
                return 0

            lax.fori_loop(0, prod_of(tree[:i]) * (dim[1] - 1), arrived, 0)
    own.wait()
    for band in range(len(plan)):
        peer = moved(me, plan[band][2][0], coord(me, plan[band][2][0]), 1 - coord(me, plan[band][2][0]))

        def sent(slot, _, band=band, peer=peer):
            copy_of(band, me, slot, peer, True).wait_send()
            return 0

        lax.fori_loop(0, dp * fsdp - 1, sent, 0)


def gather(dp, fsdp, shard):
    rows, width = shard.shape
    plan = plan_of(dp, fsdp, rows)
    n = dp * fsdp
    return pl.pallas_call(
        partial(gather_kernel, dp, fsdp, plan),
        out_shape=jax.ShapeDtypeStruct((n, rows, width), shard.dtype),
        in_specs=[pl.BlockSpec(memory_space=pl.ANY)],
        out_specs=pl.BlockSpec(memory_space=pl.ANY),
        scratch_shapes=[
            pltpu.SemaphoreType.DMA((len(plan), n)),
            pltpu.SemaphoreType.DMA((len(plan), n)),
            pltpu.SemaphoreType.DMA,
        ],
        compiler_params=pltpu.CompilerParams(collective_id=0, has_side_effects=True),
        name="gather_params",
    )(shard)


def sum_kernel(dp, fsdp, plan, x_ref, out_ref, *scratch):
    bands = len(plan)
    kept, held = scratch[:bands], scratch[bands : 2 * bands]
    send_sem, recv_sem, own_sem = scratch[2 * bands :]
    me = whoami(fsdp)
    greet(me, plan[0][2], fsdp)
    f32 = jnp.float32
    depth = len(plan[0][2])
    bases = []
    for _, _, order in plan:
        base, at = [], 0
        for i in range(depth):
            base.append(at)
            at += prod_of(order[i + 1 :]) * (order[i][1] - 1)
        bases.append(base)

    def sending(band, i, source, r, rest):
        dim = plan[band][2][i]
        mine = coord(me, dim)
        gap = dim[1] - 1
        there = lax.rem(mine + 1 + r, dim[1])
        back = lax.rem(mine - there - 1 + 2 * dim[1], dim[1])
        slot = bases[band][i] + rest * gap + back
        return pltpu.make_async_remote_copy(
            src_ref=source,
            dst_ref=held[band].at[slot],
            send_sem=send_sem.at[band, bases[band][i] + rest * gap + r],
            recv_sem=recv_sem.at[band, slot],
            device_id=place(moved(me, dim, mine, there), fsdp),
            device_id_type=MESH,
        )

    def own_copy(band, index):
        start, rows, order = plan[band]
        slab = spread(me, me, order[1:], index)
        return pltpu.make_async_copy(
            x_ref.at[slab, pl.ds(start, rows), :], kept[band].at[index], own_sem.at[band, index]
        )

    def walk(band, i, visit):
        order = plan[band][2]
        if i == depth - 1:
            visit(0, 0, 0)
            return
        dim = order[i + 1]
        inner = prod_of(order[i + 2 :])
        for r in range(dim[1]):
            at = lax.rem(coord(me, dim) + 1 + r, dim[1])

            def one(rest, _, r=r, at=at):
                visit(r, rest, at * inner + rest)
                return 0

            lax.fori_loop(0, inner, one, 0)

    for band in range(bands):
        start, rows, order = plan[band]
        core = order[0]
        mine = coord(me, core)

        def begin(r, rest, index, band=band, start=start, rows=rows, order=order, core=core, mine=mine):
            slab = moved(spread(me, me, order[1:], index), core, mine, lax.rem(mine + 1, core[1]))
            sending(band, 0, x_ref.at[slab, pl.ds(start, rows), :], 0, index).start()
            own_copy(band, index).start()

        walk(band, 0, begin)
    for i in range(depth):
        for band in range(bands):
            start, rows, order = plan[band]
            gap = order[i][1] - 1
            where = 0
            for dim in order[1 : i + 1]:
                where = where * dim[1] + coord(me, dim)
            where = where * prod_of(order[i + 1 :])

            def visit(r, rest, index, i=i, band=band, start=start, rows=rows, order=order, gap=gap, where=where):
                if i == 0:
                    own_copy(band, index).wait()
                total = kept[band][where + index].astype(f32)
                for q in range(gap):
                    slot = bases[band][i] + index * gap + q
                    pltpu.make_async_remote_copy(
                        src_ref=held[band].at[slot],
                        dst_ref=held[band].at[slot],
                        send_sem=send_sem.at[band, 0],
                        recv_sem=recv_sem.at[band, slot],
                        device_id=place(moved(me, order[0], coord(me, order[0]), 1 - coord(me, order[0])), fsdp),
                        device_id_type=MESH,
                    ).wait_recv()
                    total = total + held[band][slot].astype(f32)
                if i == depth - 1:
                    out_ref[start : start + rows, :] = total
                    return
                kept[band][where + index] = total.astype(kept[band].dtype)
                if r < order[i + 1][1] - 1:
                    sending(band, i + 1, kept[band].at[where + index], r, rest).start()

            walk(band, i, visit)
    for band in range(bands):
        start, rows, order = plan[band]

        def sent(slot, _, band=band):
            core = plan[band][2][0]
            pltpu.make_async_remote_copy(
                src_ref=held[band].at[0],
                dst_ref=held[band].at[0],
                send_sem=send_sem.at[band, slot],
                recv_sem=recv_sem.at[band, 0],
                device_id=place(moved(me, core, coord(me, core), 1 - coord(me, core)), fsdp),
                device_id_type=MESH,
            ).wait_send()
            return 0

        lax.fori_loop(0, dp * fsdp - 1, sent, 0)


def sum_shards(dp, fsdp, terms):
    n, rows, width = terms.shape
    plan = plan_of(dp, fsdp, rows)
    return pl.pallas_call(
        partial(sum_kernel, dp, fsdp, plan),
        out_shape=jax.ShapeDtypeStruct((rows, width), jnp.float32),
        in_specs=[pl.BlockSpec(memory_space=pl.ANY)],
        out_specs=pl.BlockSpec(memory_space=pltpu.VMEM),
        scratch_shapes=[pltpu.VMEM((n // 2, band[1], width), terms.dtype) for band in plan]
        + [pltpu.VMEM((n - 1, band[1], width), terms.dtype) for band in plan]
        + [
            pltpu.SemaphoreType.DMA((len(plan), n)),
            pltpu.SemaphoreType.DMA((len(plan), n)),
            pltpu.SemaphoreType.DMA((len(plan), n // 2)),
        ],
        compiler_params=pltpu.CompilerParams(
            collective_id=1, has_side_effects=True, vmem_limit_bytes=56 * 1024 * 1024
        ),
        name="sum_grads",
    )(terms)


PARAM_NAMES = [
    "query_weight",
    "key_weight",
    "value_weight",
    "query_bias",
    "value_bias",
    "out_weight",
    "out_bias",
    "first_gain",
    "first_shift",
    "up_weight",
    "up_bias",
    "down_weight",
    "down_bias",
    "second_gain",
    "second_shift",
]
VECTORS = [name for name in PARAM_NAMES if not name.endswith("_weight")]

def normalize(rows, gain, shift):
    centred = rows - jnp.mean(rows, axis=-1, keepdims=True)
    scale = lax.rsqrt(jnp.mean(centred * centred, axis=-1, keepdims=True) + 1e-06)
    normed = centred * scale
    return (normed * gain + shift, normed, scale)


def norm_back(grad, normed, scale, gain):
    scaled = grad * gain
    return scale * (
        scaled
        - jnp.mean(scaled, axis=-1, keepdims=True)
        - normed * jnp.mean(scaled * normed, axis=-1, keepdims=True)
    )


def rowdot(left, right):
    return jnp.einsum("ti,to->io", left, right, preferred_element_type=jnp.float32)


def backdot(left, right):
    return jnp.einsum("to,io->ti", left, right, preferred_element_type=jnp.float32)


def on_device(
    dp,
    fsdp,
    tokens,
    query_weight,
    key_weight,
    value_weight,
    query_bias,
    value_bias,
    out_weight,
    out_bias,
    first_gain,
    first_shift,
    up_weight,
    up_bias,
    down_weight,
    down_bias,
    second_gain,
    second_shift,
    segment_ids,
    out_grad,
):
    bf16 = jnp.bfloat16
    width = tokens.shape[1]
    n = dp * fsdp
    given = dict(
        query_bias=query_bias,
        value_bias=value_bias,
        out_bias=out_bias,
        first_gain=first_gain,
        first_shift=first_shift,
        up_bias=up_bias,
        down_bias=down_bias,
        second_gain=second_gain,
        second_shift=second_shift,
    )
    part = query_weight.shape[0]
    wide = up_weight.shape[1] // width
    tall = down_weight.shape[0]
    flat = jnp.concatenate([given[name] for name in VECTORS])
    used = (4 + wide) * part + tall
    lines = -(-flat.shape[0] // width)
    total_rows = -(-(used + lines) // TILE) * TILE
    flat = jnp.pad(flat, (0, (total_rows - used) * width - flat.shape[0])).reshape(-1, width)
    shard = jnp.concatenate(
        [query_weight, key_weight, value_weight, out_weight]
        + [up_weight[:, j * width : (j + 1) * width] for j in range(wide)]
        + [down_weight, flat],
        axis=0,
    )
    slabs = gather(dp, fsdp, shard)

    def matrix(k):
        return slabs[:, k * part : (k + 1) * part, :].reshape(n * part, width)

    params = dict(
        query_weight=matrix(0),
        key_weight=matrix(1),
        value_weight=matrix(2),
        out_weight=matrix(3),
        up_weight=jnp.concatenate([matrix(4 + j) for j in range(wide)], axis=1),
        down_weight=slabs[:, (4 + wide) * part : used, :].reshape(n * tall, width),
    )
    flat = slabs[:, used : used + lines, :].reshape(n, lines * width)
    at = 0
    for name in VECTORS:
        count = given[name].shape[0]
        params[name] = flat[:, at : at + count].reshape(-1)
        at += count
    length = tokens.shape[0]
    width = tokens.shape[1]
    heads = width // HD
    f32 = jnp.float32
    bf16 = jnp.bfloat16

    def split_heads(rows):
        return rows.reshape(length, heads, HD)

    query = (
        jnp.dot(tokens, params["query_weight"], preferred_element_type=f32)
        + params["query_bias"].astype(f32)
    ).astype(bf16)
    keys = jnp.dot(tokens, params["key_weight"], preferred_element_type=f32).astype(bf16)
    values = (
        jnp.dot(tokens, params["value_weight"], preferred_element_type=f32)
        + params["value_bias"].astype(f32)
    ).astype(bf16)
    same = (segment_ids[0][:, None] == segment_ids[0][None, :])[None]
    scores = (
        jnp.einsum(
            "qhd,khd->hqk", split_heads(query), split_heads(keys), preferred_element_type=f32
        )
        * 0.125
    )
    masked = jnp.where(same, scores, -1e30)
    top = jnp.max(masked, axis=-1, keepdims=True)
    expo = jnp.exp(masked - top)
    total = jnp.sum(expo, axis=-1, keepdims=True)
    probs = expo / total
    probs_low = probs.astype(bf16)
    attended = (
        jnp.einsum("hqk,khd->qhd", probs_low, split_heads(values), preferred_element_type=f32)
        .reshape(length, width)
        .astype(bf16)
    )
    branch = jnp.dot(attended, params["out_weight"], preferred_element_type=f32) + params[
        "out_bias"
    ].astype(f32)
    gain_first = params["first_gain"].astype(f32)
    first, normed_first, scale_first = normalize(
        tokens.astype(f32) + branch, gain_first, params["first_shift"].astype(f32)
    )
    first_low = first.astype(bf16)
    hidden = jnp.dot(first_low, params["up_weight"], preferred_element_type=f32) + params[
        "up_bias"
    ].astype(f32)
    active_full, gelu_back = jax.vjp(partial(jax.nn.gelu, approximate=False), hidden)
    active = active_full.astype(bf16)
    second_in = (
        first
        + jnp.dot(active, params["down_weight"], preferred_element_type=f32)
        + params["down_bias"].astype(f32)
    )
    gain_second = params["second_gain"].astype(f32)
    result, normed_second, scale_second = normalize(
        second_in, gain_second, params["second_shift"].astype(f32)
    )
    layer_output = result.astype(bf16)
    grad_out = out_grad.astype(f32)
    grads = {}
    grads["second_gain"] = jnp.sum(grad_out * normed_second, axis=0)
    grads["second_shift"] = jnp.sum(grad_out, axis=0)
    d_second = norm_back(grad_out, normed_second, scale_second, gain_second)
    d_down = d_second.astype(bf16)
    grads["down_bias"] = jnp.sum(d_down.astype(f32), axis=0)
    grads["down_weight"] = rowdot(active, d_down)
    d_hidden = gelu_back(backdot(d_down, params["down_weight"]))[0].astype(bf16)
    grads["up_bias"] = jnp.sum(d_hidden.astype(f32), axis=0)
    grads["up_weight"] = rowdot(first_low, d_hidden)
    d_first = d_second + backdot(d_hidden, params["up_weight"])
    grads["first_gain"] = jnp.sum(d_first * normed_first, axis=0)
    grads["first_shift"] = jnp.sum(d_first, axis=0)
    d_branch_full = norm_back(d_first, normed_first, scale_first, gain_first)
    d_branch = d_branch_full.astype(bf16)
    grads["out_bias"] = jnp.sum(d_branch.astype(f32), axis=0)
    grads["out_weight"] = rowdot(attended, d_branch)
    d_attended = split_heads(backdot(d_branch, params["out_weight"]).astype(bf16))
    d_probs = jnp.einsum(
        "qhd,khd->hqk", d_attended, split_heads(values), preferred_element_type=f32
    )
    d_scores = (probs * (d_probs - jnp.sum(d_probs * probs, axis=-1, keepdims=True))).astype(bf16)
    d_query = (
        (
            jnp.einsum("hqk,khd->qhd", d_scores, split_heads(keys), preferred_element_type=f32)
            * 0.125
        )
        .reshape(length, width)
        .astype(bf16)
    )
    d_keys = (
        (
            jnp.einsum("hqk,qhd->khd", d_scores, split_heads(query), preferred_element_type=f32)
            * 0.125
        )
        .reshape(length, width)
        .astype(bf16)
    )
    d_values = (
        jnp.einsum("hqk,qhd->khd", probs_low, d_attended, preferred_element_type=f32)
        .reshape(length, width)
        .astype(bf16)
    )
    grads["query_weight"] = rowdot(tokens, d_query)
    grads["key_weight"] = rowdot(tokens, d_keys)
    grads["value_weight"] = rowdot(tokens, d_values)
    grads["query_bias"] = jnp.sum(d_query.astype(f32), axis=0)
    grads["value_bias"] = jnp.sum(d_values.astype(f32), axis=0)
    input_grad = (
        d_branch_full
        + backdot(d_query, params["query_weight"])
        + backdot(d_keys, params["key_weight"])
        + backdot(d_values, params["value_weight"])
    )
    def by_owner(value):
        return value.astype(bf16).reshape(n, -1, width)

    flat = jnp.concatenate(
        [grads[name].astype(bf16).reshape(n, -1) for name in VECTORS], axis=1
    )
    flat = jnp.pad(flat, ((0, 0), (0, (total_rows - used) * width - flat.shape[1])))
    up = grads["up_weight"].astype(bf16)
    terms = jnp.concatenate(
        [by_owner(grads[name + "_weight"]) for name in ("query", "key", "value", "out")]
        + [by_owner(up[:, j * width : (j + 1) * width]) for j in range(wide)]
        + [by_owner(grads["down_weight"]), flat.reshape(n, -1, width)],
        axis=1,
    )
    sums = sum_shards(dp, fsdp, terms)
    owned = {}
    for k, name in enumerate(("query", "key", "value", "out")):
        owned[name + "_weight"] = sums[k * part : (k + 1) * part]
    owned["up_weight"] = jnp.concatenate(
        [sums[(4 + j) * part : (5 + j) * part] for j in range(wide)], axis=1
    )
    owned["down_weight"] = sums[(4 + wide) * part : used]
    flat = sums[used : used + lines].reshape(-1)
    at = 0
    for name in VECTORS:
        count = given[name].shape[0]
        owned[name] = flat[at : at + count]
        at += count
    return tuple([layer_output, input_grad] + [owned[name] for name in PARAM_NAMES])


def solution(mesh):
    in_specs = (
        P(("dp", "fsdp"), None),
        P(("dp", "fsdp"), None),
        P(("dp", "fsdp"), None),
        P(("dp", "fsdp"), None),
        P(("dp", "fsdp")),
        P(("dp", "fsdp")),
        P(("dp", "fsdp"), None),
        P(("dp", "fsdp")),
        P(("dp", "fsdp")),
        P(("dp", "fsdp")),
        P(("dp", "fsdp"), None),
        P(("dp", "fsdp")),
        P(("dp", "fsdp"), None),
        P(("dp", "fsdp")),
        P(("dp", "fsdp")),
        P(("dp", "fsdp")),
        P(("dp", "fsdp"), None),
        P(("dp", "fsdp"), None),
    )
    out_specs = (
        P(("dp", "fsdp"), None),
        P(("dp", "fsdp"), None),
        P(("dp", "fsdp"), None),
        P(("dp", "fsdp"), None),
        P(("dp", "fsdp"), None),
        P(("dp", "fsdp")),
        P(("dp", "fsdp")),
        P(("dp", "fsdp"), None),
        P(("dp", "fsdp")),
        P(("dp", "fsdp")),
        P(("dp", "fsdp")),
        P(("dp", "fsdp"), None),
        P(("dp", "fsdp")),
        P(("dp", "fsdp"), None),
        P(("dp", "fsdp")),
        P(("dp", "fsdp")),
        P(("dp", "fsdp")),
    )
    return jax.shard_map(
        partial(on_device, mesh.shape["dp"], mesh.shape["fsdp"]),
        mesh=mesh,
        in_specs=in_specs,
        out_specs=out_specs,
        check_vma=False,
    )
```

profile of v0, /device:TPU:0, one launch (start us, length us, event | category | flops | bytes accessed | tf_op | source)
XLA Modules:
  0.0 323.1 jit_solution(13694527552844397029)
XLA Ops:
  6.8 0.9 constant_dynamic-update-slice_fusion.1
  7.7 6.1 %concatenate.18 = bf16[288]{0:T(512)(128)(2,1)S(1)} concatenate(bf16[24]{0:T(256)(128)(2,1)} %param.22, bf16[24]{0:T(256)(128)(2,1)} %param.23, bf16[24]{0:T(256)(128)(2,1)} %param.25, bf16[24]{0:T(256)(128)(2,1)} %param.26, bf16[24]{0:T(256)(128)(2,1)} %param.27, bf16[96]{0:T(256)(128)(2,1)} %param.29, bf16[24]{0:T(256)(128)(2,1)} %param.31, bf16[24]{0:T(256)(128)(2,1)} %param.32, ...), dimensions={0} | concatenate | bytes 1152 | tf_op jit(solution)/shard_map/concatenate | solution.py:397
  14.7 109.6 %gather_params.1 = bf16[32,304,768]{2,1,0:T(8,128)(2,1)} custom-call(bf16[304,768]{1,0:T(8,128)(2,1)} %copy-done.26), custom_call_target="tpu_custom_call" | custom-call | tf_op jit(solution)/shard_map/gather_params/pallas_call | solution.py:162
  124.3 1.1 slice.177
  126.3 6.7 %fusion.42 = (bf16[32,24,768]{2,1,0:T(8,128)(2,1)}, bf16[32,24,768]{2,1,0:T(8,128)(2,1)}, bf16[32,24,768]{2,1,0:T(8,128)(2,1)}, bf16[32,24,768]{2,1,0:T(8,128)(2...) fusion(bf16[32,304,768]{2,1,0:T(8,128)(2,1)} %gather_params.1), kind=kLoop, calls=%fused_computation.138 | loop fusion | bytes 18874368 | tf_op jit(solution)/shard_map/slice | solution.py:411
  133.8 1.8 fusion.13
  136.2 1.3 fusion.45
  138.2 1.8 fusion.46
  140.4 9.3 %multiply_convert_fusion = (bf16[128,3072]{1,0:T(8,128)(2,1)S(1)}, f32[128,3072]{1,0:T(8,128)}, f32[128,3072]{1,0:T(8,128)}) fusion(f32[3072]{0:T(1024)S(1)} %reshape.346, bf16[768,768]{1,0:T(8,128)(2,1)} %bitcast.139, bf16[768,768]{1,0:T(8,128)(2,1)} %bitcast.141, bf16[768,768]{1,0:T(8,128)(2,1)} %bitcast.143, bf16[768,768]{1,0:T(8,128)(2,1)} %bitcast.145, ...), kind=kOutput, calls=%fused_computation.8 | convolution fusion | flops 649297920 | bytes 9063424 | tf_op jit(solution)/shard_map/dot_general | solution.py:471
  149.6 2.9 slice.191
  152.6 0.9 fusion.47
  153.5 1.2 copy-done
  157.1 2.3 fusion.22
  159.3 1.5 convert_reduce_fusion.1
  160.9 5.4 %fusion.48 = (bf16[3072]{0:T(1024)(128)(2,1)}, bf16[128,3072]{1,0:T(8,128)(2,1)S(1)}) fusion(f32[128,3072]{1,0:T(8,128)S(1)} %copy-done.46, f32[128,3072]{1,0:T(8,128)} %get-tuple-element.72, bf16[3072,768]{1,0:T(8,128)(2,1)} %bitcast.116, f32[128,768]{1,0:T(8,128)S(1)} %get-tuple-element.25), kind=kOutput, calls=%fused_computation.144 | convolution fusion | flops 609973248 | bytes 9050112 | tf_op jit(solution)/shard_map/to,io->ti/dot_general | solution.py:355
  166.3 2.3 multiply_reduce_fusion.1
  171.3 1.7 multiply_reduce_fusion
  176.0 1.3 convolution_add_fusion.2
  177.3 2.5 bitcast_reduce_fusion
  179.9 1.3 convolution_add_fusion.1
  181.7 0.8 copy-done.8
  185.2 1.0 copy-done.17
  186.2 1.5 convolution_convert_fusion.1
  188.4 1.0 copy-done.6
  189.5 1.7 convolution_convert_fusion
  191.6 5.3 %copy-done.1 = bf16[32,304,768]{2,1,0:T(8,128)(2,1)} copy-done((bf16[32,304,768]{2,1,0:T(8,128)(2,1)}, bf16[32,304,768]{2,1,0:T(8,128)(2,1)S(1)}, u32[]{:S(2)}) %copy-start.1) | copy-done | bytes 14942232
  198.1 0.9 constant_dynamic-update-slice_fusion.10.x_ref
  199.0 117.0 %sum_grads.1 = f32[304,768]{1,0:T(8,128)} custom-call(bf16[32,304,768]{2,1,0:T(8,128)(2,1)} %constant_dynamic-update-slice_fusion.10.x_ref), custom_call_target="tpu_custom_call" | custom-call | tf_op jit(solution)/shard_map/sum_grads/pallas_call | solution.py:296
  316.1 1.9 fusion.44
  317.9 1.5 slice_bitcast_fusion
  320.1 1.3 slice_bitcast_fusion.3
  321.4 1.7 slice.219
  (159 shorter events, 24.2 us)
Async XLA Ops:
  126.3 6.8 %copy-start.4 = (bf16[128,768]{1,0:T(8,128)(2,1)S(1)}, bf16[128,768]{1,0:T(8,128)(2,1)}, u32[]{:S(2)}) copy-start(bf16[128,768]{1,0:T(8,128)(2,1)} %param.18) | copy-start | bytes 589828
  133.6 3.9 %copy-start.27 = (bf16[768,128]{1,0:T(8,128)(2,1)}, bf16[768,128]{1,0:T(8,128)(2,1)S(1)}, u32[]{:S(2)}) copy-start(bf16[768,128]{1,0:T(8,128)(2,1)S(1)} %fusion.12) | copy-start | bytes 589828
  133.7 2.3 copy-start.45
  135.5 2.0 copy-start.20
  136.1 2.1 copy-start.22
  136.2 2.0 copy-start.28
  138.2 11.5 %copy-start.18 = (bf16[12,64,128]{2,1,0:T(8,128)(2,1)}, bf16[12,64,128]{2,1,0:T(8,128)(2,1)S(1)}, u32[]{:S(2)}) copy-start(bf16[12,64,128]{2,1,0:T(8,128)(2,1)S(1)} %convolution_convert_fusion.8) | copy-start | bytes 589828
  140.2 12.4 %copy-start.29 = (f32[128]{0:T(128)}, f32[128]{0:T(128)S(1)}, u32[]{:S(2)}) copy-start(f32[128]{0:T(128)S(1)} %broadcast_multiply_fusion.5) | copy-start | bytes 1540
  140.4 12.2 %copy-start.33 = (f32[128]{0:T(128)}, f32[128]{0:T(128)S(1)}, u32[]{:S(2)}) copy-start(f32[128]{0:T(128)S(1)} %add_rsqrt_fusion.1) | copy-start | bytes 1540
  149.6 3.0 copy-start.5
  152.6 2.1 copy-start
  152.6 4.4 %copy-start.25 = (bf16[128,768]{1,0:T(8,128)(2,1)S(1)}, bf16[128,768]{1,0:T(8,128)(2,1)}, u32[]{:S(2)}) copy-start(bf16[128,768]{1,0:T(8,128)(2,1)} %param.35) | copy-start | bytes 589828
  157.0 3.8 %copy-start.46 = (f32[128,3072]{1,0:T(8,128)S(1)}, f32[128,3072]{1,0:T(8,128)}, u32[]{:S(2)}) copy-start(f32[128,3072]{1,0:T(8,128)} %get-tuple-element.29) | copy-start | bytes 4718596
  160.8 5.5 %copy-start.9 = (f32[128,768]{1,0:T(8,128)}, f32[128,768]{1,0:T(8,128)S(1)}, u32[]{:S(2)}) copy-start(f32[128,768]{1,0:T(8,128)S(1)} %get-tuple-element.25) | copy-start | bytes 1179652
  160.8 5.5 %copy-start.12 = (bf16[32,24,768]{2,1,0:T(8,128)(2,1)S(1)}, bf16[32,24,768]{2,1,0:T(8,128)(2,1)}, u32[]{:S(2)}) copy-start(bf16[32,24,768]{2,1,0:T(8,128)(2,1)} %get-tuple-element.31) | copy-start | bytes 3538948
  160.8 5.5 %copy-start.13 = (bf16[32,24,768]{2,1,0:T(8,128)(2,1)S(1)}, bf16[32,24,768]{2,1,0:T(8,128)(2,1)}, u32[]{:S(2)}) copy-start(bf16[32,24,768]{2,1,0:T(8,128)(2,1)} %get-tuple-element.32) | copy-start | bytes 3538948
  160.8 5.5 %copy-start.14 = (bf16[32,24,768]{2,1,0:T(8,128)(2,1)S(1)}, bf16[32,24,768]{2,1,0:T(8,128)(2,1)}, u32[]{:S(2)}) copy-start(bf16[32,24,768]{2,1,0:T(8,128)(2,1)} %get-tuple-element.33) | copy-start | bytes 3538948
  160.8 5.5 %copy-start.15 = (bf16[32,24,768]{2,1,0:T(8,128)(2,1)S(1)}, bf16[32,24,768]{2,1,0:T(8,128)(2,1)}, u32[]{:S(2)}) copy-start(bf16[32,24,768]{2,1,0:T(8,128)(2,1)} %get-tuple-element.34) | copy-start | bytes 3538948
  160.8 5.5 %copy-start.30 = (f32[128]{0:T(128)S(1)}, f32[128]{0:T(128)}, u32[]{:S(2)}) copy-start(f32[128]{0:T(128)} %copy-done.29) | copy-start | bytes 1540
  160.9 5.5 %copy-start.34 = (f32[128]{0:T(128)S(1)}, f32[128]{0:T(128)}, u32[]{:S(2)}) copy-start(f32[128]{0:T(128)} %copy-done.33) | copy-start | bytes 1540
  166.3 2.4 copy-start.16
  171.3 1.8 copy-start.32
  177.3 2.5 copy-start.11
  191.2 5.8 %copy-start.42 = (bf16[12,64]{1,0:T(8,128)(2,1)S(1)}, bf16[12,64]{1,0:T(8,128)(2,1)}, u32[]{:S(2)}) copy-start(bf16[12,64]{1,0:T(8,128)(2,1)} %get-tuple-element.80) | copy-start | bytes 4612
  191.2 5.8 %copy-start.39 = (bf16[768]{0:T(1024)(128)(2,1)S(1)}, bf16[768]{0:T(1024)(128)(2,1)}, u32[]{:S(2)}) copy-start(bf16[768]{0:T(1024)(128)(2,1)} %get-tuple-element.26) | copy-start | bytes 4612
  191.2 5.9 %copy-start.44 = (bf16[768]{0:T(1024)(128)(2,1)S(1)}, bf16[768]{0:T(1024)(128)(2,1)}, u32[]{:S(2)}) copy-start(bf16[768]{0:T(1024)(128)(2,1)} %get-tuple-element.17) | copy-start | bytes 4612
  191.2 6.0 %copy-start.43 = (bf16[768]{0:T(1024)(128)(2,1)S(1)}, bf16[768]{0:T(1024)(128)(2,1)}, u32[]{:S(2)}) copy-start(bf16[768]{0:T(1024)(128)(2,1)} %get-tuple-element.22) | copy-start | bytes 4612
  191.2 6.1 %copy-start.40 = (bf16[3072]{0:T(1024)(128)(2,1)S(1)}, bf16[3072]{0:T(1024)(128)(2,1)}, u32[]{:S(2)}) copy-start(bf16[3072]{0:T(1024)(128)(2,1)} %get-tuple-element.82) | copy-start | bytes 18436
  191.2 6.2 %copy-start.38 = (bf16[768]{0:T(1024)(128)(2,1)S(1)}, bf16[768]{0:T(1024)(128)(2,1)}, u32[]{:S(2)}) copy-start(bf16[768]{0:T(1024)(128)(2,1)} %get-tuple-element.24) | copy-start | bytes 4612
  191.3 6.3 %copy-start.36 = (bf16[768]{0:T(1024)(128)(2,1)S(1)}, bf16[768]{0:T(1024)(128)(2,1)}, u32[]{:S(2)}) copy-start(bf16[768]{0:T(1024)(128)(2,1)} %get-tuple-element.19) | copy-start | bytes 4612
  191.3 6.4 %copy-start.37 = (bf16[768]{0:T(1024)(128)(2,1)S(1)}, bf16[768]{0:T(1024)(128)(2,1)}, u32[]{:S(2)}) copy-start(bf16[768]{0:T(1024)(128)(2,1)} %get-tuple-element.59) | copy-start | bytes 4612
  191.6 5.3 %copy-start.1 = (bf16[32,304,768]{2,1,0:T(8,128)(2,1)}, bf16[32,304,768]{2,1,0:T(8,128)(2,1)S(1)}, u32[]{:S(2)}) copy-start(bf16[32,304,768]{2,1,0:T(8,128)(2,1)S(1)} %constant_dynamic-update-slice_fusion.11) | copy-start | bytes 44826628
  (15 other events, 15.6 us)
where the time goes:
time: 326 us; the launch traced here: 323 us
  Pallas kernels  227 us (70%)
  local copies, waits for them, and re-layouts  49.7 us (15%)
  matrix products  38.1 us (12%)
  other arithmetic  7.16 us (2%)
    pallas_call x1, Pallas kernels, sum_shards(): pl.pallas_call(partial(sum_kernel, dp, fsdp, plan), out_shape=jax.ShapeDt...  117 us
    pallas_call x1, Pallas kernels, gather(): pl.pallas_call(partial(gather_kernel, dp, fsdp, plan), out_shape=jax.Shap...  110 us
    unnamed x114, local copies, waits for them, and re-layouts  21.4 us
    dot_general x6, matrix products, backdot(): jnp.einsum('to,io->ti', left, right, preferred_element_type=jnp.float32)  11.4 us
    dot_general x1, matrix products, on_device(): jnp.dot(first_low, params['up_weight'], preferred_element_type=f32)  9.25 us
    slice x1, local copies, waits for them, and re-layouts, matrix(): return slabs[:, k * part:(k + 1) * part, :].reshape(n * part, width)  6.66 us

commit v1 on v0

--- a/solution.py
+++ b/solution.py
@@ -30,14 +30,13 @@
 def plan_of(dp, fsdp, rows):
     core, links = dims_of(dp, fsdp)
     tiles = rows // TILE
-    if len(links) != 3 or tiles < 3:
+    if len(links) != 3 or tiles < 2:
         return [(0, rows, [core] + links)]
     y, x, z = links
-    outer = max(1, (tiles * 3 + 4) // 8)
-    inner = tiles - 2 * outer
-    orders = [[core, y, x, z], [core, z, y, x], [core, x, z, y]]
+    most = max(1, min(tiles - 1, (tiles * 7 + 5) // 11))
+    orders = [[core, y, x, z], [core, x, z, y]]
     plan, start = [], 0
-    for count, order in zip((outer, inner, outer), orders):
+    for count, order in zip((most, tiles - most), orders):
         plan.append((start * TILE, count * TILE, order))
         start += count
     return plan
@@ -85,8 +84,14 @@
     pl.semaphore_wait(barrier, count)
 
 
-def gather_kernel(dp, fsdp, plan, x_ref, out_ref, send_sem, recv_sem, own_sem):
+def gather_kernel(dp, fsdp, plan, *refs):
+    *parts, out_ref, x_ref, send_sem, recv_sem, own_sem = refs
     me = whoami(fsdp)
+    blocks, width = [], x_ref.shape[1]
+    for ref in parts:
+        for j in range(ref.shape[1] // width):
+            blocks.append(ref[:, j * width : (j + 1) * width].astype(jnp.float32))
+    x_ref[...] = jnp.concatenate(blocks, axis=0).astype(x_ref.dtype)
     greet(me, plan[0][2], fsdp)
     own = pltpu.make_async_copy(x_ref, out_ref.at[me], own_sem)
     own.start()
@@ -106,7 +111,7 @@
 
     bases = []
     for _, _, order in plan:
-        tree = order[1:] + order[:1]
+        tree = order[:0:-1] + order[:1]
         base, at = {}, 0
         for i in range(-1, len(tree)):
             arrivals = 1 if i < 0 else prod_of(tree[:i]) * (tree[i][1] - 1)
@@ -118,7 +123,7 @@
     for i in range(-1, depth):
         for band in range(len(plan)):
             order = plan[band][2]
-            tree = order[1:] + order[:1]
+            tree = order[:0:-1] + order[:1]
 
             def sends(slab, k, act, i=i, band=band, tree=tree):
                 for j in range(i + 1, depth):
@@ -155,23 +160,23 @@
         lax.fori_loop(0, dp * fsdp - 1, sent, 0)
 
 
-def gather(dp, fsdp, shard):
-    rows, width = shard.shape
+def gather(dp, fsdp, parts, rows, width):
     plan = plan_of(dp, fsdp, rows)
     n = dp * fsdp
     return pl.pallas_call(
         partial(gather_kernel, dp, fsdp, plan),
-        out_shape=jax.ShapeDtypeStruct((n, rows, width), shard.dtype),
-        in_specs=[pl.BlockSpec(memory_space=pl.ANY)],
+        out_shape=jax.ShapeDtypeStruct((n, rows, width), parts[0].dtype),
+        in_specs=[pl.BlockSpec(memory_space=pltpu.VMEM)] * len(parts),
         out_specs=pl.BlockSpec(memory_space=pl.ANY),
         scratch_shapes=[
+            pltpu.VMEM((rows, width), parts[0].dtype),
             pltpu.SemaphoreType.DMA((len(plan), n)),
             pltpu.SemaphoreType.DMA((len(plan), n)),
             pltpu.SemaphoreType.DMA,
         ],
-        compiler_params=pltpu.CompilerParams(collective_id=0, has_side_effects=True),
+        compiler_params=pltpu.CompilerParams(collective_id=0, has_side_effects=True, vmem_limit_bytes=6 * 1024 * 1024),
         name="gather_params",
-    )(shard)
+    )(*parts)
 
 
 def sum_kernel(dp, fsdp, plan, x_ref, out_ref, *scratch):
@@ -306,7 +311,7 @@
             pltpu.SemaphoreType.DMA((len(plan), n // 2)),
         ],
         compiler_params=pltpu.CompilerParams(
-            collective_id=1, has_side_effects=True, vmem_limit_bytes=56 * 1024 * 1024
+            collective_id=1, has_side_effects=True, vmem_limit_bytes=28 * 1024 * 1024 if n <= 64 else 56 * 1024 * 1024
         ),
         name="sum_grads",
     )(terms)
@@ -394,18 +399,20 @@
     part = query_weight.shape[0]
     wide = up_weight.shape[1] // width
     tall = down_weight.shape[0]
-    flat = jnp.concatenate([given[name] for name in VECTORS])
     used = (4 + wide) * part + tall
-    lines = -(-flat.shape[0] // width)
+    lines = len(VECTORS)
     total_rows = -(-(used + lines) // TILE) * TILE
-    flat = jnp.pad(flat, (0, (total_rows - used) * width - flat.shape[0])).reshape(-1, width)
-    shard = jnp.concatenate(
-        [query_weight, key_weight, value_weight, out_weight]
-        + [up_weight[:, j * width : (j + 1) * width] for j in range(wide)]
-        + [down_weight, flat],
-        axis=0,
-    )
-    slabs = gather(dp, fsdp, shard)
+    row = lax.broadcasted_iota(jnp.int32, (total_rows - used, width), 0)
+    flat = jnp.zeros((total_rows - used, width), jnp.float32)
+    for k, name in enumerate(VECTORS):
+        padded = jnp.pad(given[name].astype(jnp.float32), (0, width - given[name].shape[0]))
+        flat = jnp.where(row == k, padded[None, :], flat)
+    flat = flat.astype(bf16)
+    parts = [query_weight, key_weight, value_weight, out_weight, up_weight, down_weight, flat]
+    if part % 8 or tall % 8:
+        wides = [up_weight[:, j * width : (j + 1) * width] for j in range(wide)]
+        parts = [jnp.concatenate(parts[:4] + wides + parts[5:], axis=0)]
+    slabs = gather(dp, fsdp, parts, total_rows, width)
 
     def matrix(k):
         return slabs[:, k * part : (k + 1) * part, :].reshape(n * part, width)
@@ -418,12 +425,8 @@
         up_weight=jnp.concatenate([matrix(4 + j) for j in range(wide)], axis=1),
         down_weight=slabs[:, (4 + wide) * part : used, :].reshape(n * tall, width),
     )
-    flat = slabs[:, used : used + lines, :].reshape(n, lines * width)
-    at = 0
-    for name in VECTORS:
-        count = given[name].shape[0]
-        params[name] = flat[:, at : at + count].reshape(-1)
-        at += count
+    for k, name in enumerate(VECTORS):
+        params[name] = slabs[:, used + k, : given[name].shape[0]].reshape(-1)
     length = tokens.shape[0]
     width = tokens.shape[1]
     heads = width // HD
@@ -541,15 +544,18 @@
     def by_owner(value):
         return value.astype(bf16).reshape(n, -1, width)
 
-    flat = jnp.concatenate(
-        [grads[name].astype(bf16).reshape(n, -1) for name in VECTORS], axis=1
-    )
-    flat = jnp.pad(flat, ((0, 0), (0, (total_rows - used) * width - flat.shape[1])))
+    row = lax.broadcasted_iota(jnp.int32, (n, total_rows - used, width), 1)
+    flat = jnp.zeros((n, total_rows - used, width), f32)
+    for k, name in enumerate(VECTORS):
+        mine = grads[name].reshape(n, -1)
+        mine = jnp.pad(mine, ((0, 0), (0, width - mine.shape[1])))
+        flat = jnp.where(row == k, mine[:, None, :], flat)
+    flat = flat.astype(bf16)
     up = grads["up_weight"].astype(bf16)
     terms = jnp.concatenate(
         [by_owner(grads[name + "_weight"]) for name in ("query", "key", "value", "out")]
         + [by_owner(up[:, j * width : (j + 1) * width]) for j in range(wide)]
-        + [by_owner(grads["down_weight"]), flat.reshape(n, -1, width)],
+        + [by_owner(grads["down_weight"]), flat],
         axis=1,
     )
     sums = sum_shards(dp, fsdp, terms)
@@ -560,12 +566,8 @@
         [sums[(4 + j) * part : (5 + j) * part] for j in range(wide)], axis=1
     )
     owned["down_weight"] = sums[(4 + wide) * part : used]
-    flat = sums[used : used + lines].reshape(-1)
-    at = 0
-    for name in VECTORS:
-        count = given[name].shape[0]
-        owned[name] = flat[at : at + count]
-        at += count
+    for k, name in enumerate(VECTORS):
+        owned[name] = sums[used + k, : given[name].shape[0]]
     return tuple([layer_output, input_grad] + [owned[name] for name in PARAM_NAMES])
 
 

time: 326 us -> 308 us (0.945)
  Pallas kernels: 227 us -> 198 us
  other arithmetic: 7.16 us -> 11.9 us
    pallas_call x1, Pallas kernels: 110 us -> 71.8 us  [gather(): pl.pallas_call(partial(gather_kernel, dp, fsdp, plan), out_shape=jax.Shap...]
    pallas_call x1, Pallas kernels: 117 us -> 126 us  [sum_shards(): pl.pallas_call(partial(sum_kernel, dp, fsdp, plan), out_shape=jax.ShapeDt...]
    concatenate x4 -> x0, local copies, waits for them, and re-layouts: 7.17 us -> none  [the longest x1 6.11 us: on_device(): flat = jnp.concatenate([given[name] for name in VECTORS])]
    unnamed x114 -> x159, local copies, waits for them, and re-layouts: 21.4 us -> 27.4 us
    slice x3 -> x0, local copies, waits for them, and re-layouts: 3.79 us -> none  [the longest x2 2.74 us: on_device(): owned[name] = flat[at:at + count]]
    pad x2 -> x14, local copies, waits for them, and re-layouts: 0.06 us -> 3.45 us  [the longest x5 3.36 us: on_device(): jnp.pad(given[name].astype(jnp.float32), (0, width - given[name].shape[0]))]
where the time goes in v1:
time: 308 us; the launch traced here: 303 us
  Pallas kernels  198 us (64%)
  local copies, waits for them, and re-layouts  51.2 us (17%)
  matrix products  39.8 us (13%)
  other arithmetic  11.9 us (4%)
    pallas_call x1, Pallas kernels, sum_shards(): pl.pallas_call(partial(sum_kernel, dp, fsdp, plan), out_shape=jax.ShapeDt...  126 us
    pallas_call x1, Pallas kernels, gather(): pl.pallas_call(partial(gather_kernel, dp, fsdp, plan), out_shape=jax.Shap...  71.8 us
    unnamed x159, local copies, waits for them, and re-layouts  27.4 us
    dot_general x6, matrix products, backdot(): jnp.einsum('to,io->ti', left, right, preferred_element_type=jnp.float32)  11.7 us
    dot_general x1, matrix products, on_device(): jnp.dot(first_low, params['up_weight'], preferred_element_type=f32)  9.24 us
    slice x1, local copies, waits for them, and re-layouts, matrix(): return slabs[:, k * part:(k + 1) * part, :].reshape(n * part, width)  6.42 us

profile of v1, /device:TPU:0, one launch (start us, length us, event | category | flops | bytes accessed | tf_op | source)
XLA Modules:
  0.0 302.7 jit_solution(17400875807604175498)
XLA Ops:
  10.2 71.8 %gather_params.1 = bf16[32,304,768]{2,1,0:T(8,128)(2,1)S(1)} custom-call(bf16[24,768]{1,0:T(8,128)(2,1)S(1)} %copy-done.3, bf16[24,768]{1,0:T(8,128)(2,1)S(1)} %copy-done.4, bf16[24,768]{1,0:T(8,128)(2,1)S(1)} %copy-done.5, bf16[24,768]{1,0:T(8,128)(2,1)S(1)} %copy-done.6, bf16[24,3072]{1,0:T(8,128)(2,1)S(1)} %copy-done.1, bf16[96,768]{1,0:T(8,128)(2,1)S(1)} %copy-done.2, ...), custom_call_target="tpu_custom_call" | custom-call | tf_op jit(solution)/shard_map/gather_params/pallas_call | solution.py:166
  82.1 5.3 %copy-done = bf16[32,304,768]{2,1,0:T(8,128)(2,1)} copy-done((bf16[32,304,768]{2,1,0:T(8,128)(2,1)}, bf16[32,304,768]{2,1,0:T(8,128)(2,1)S(1)}, u32[]{:S(2)}) %copy-start) | copy-done | bytes 14942232
  90.6 6.4 %fusion.43 = (bf16[32,24,768]{2,1,0:T(8,128)(2,1)}, bf16[32,24,768]{2,1,0:T(8,128)(2,1)}, bf16[32,24,768]{2,1,0:T(8,128)(2,1)}, bf16[32,24,768]{2,1,0:T(8,128)(2...) fusion(bf16[32,304,768]{2,1,0:T(8,128)(2,1)} %copy-done), kind=kLoop, calls=%fused_computation.149 | loop fusion | bytes 18874368 | tf_op jit(solution)/shard_map/slice | solution.py:418
  97.0 1.4 reshape.333
  98.4 1.4 reshape.331
  99.8 2.1 fusion.12
  102.6 2.2 fusion.13
  105.7 1.3 fusion.46
  108.0 1.7 fusion.47
  110.1 9.2 %multiply_convert_fusion = (bf16[128,3072]{1,0:T(8,128)(2,1)S(1)}, f32[128,3072]{1,0:T(8,128)}, f32[128,3072]{1,0:T(8,128)}) fusion(f32[3072]{0:T(1024)S(1)} %copy-done.42, bf16[768,768]{1,0:T(8,128)(2,1)} %bitcast.136, bf16[768,768]{1,0:T(8,128)(2,1)} %bitcast.138, bf16[768,768]{1,0:T(8,128)(2,1)} %bitcast.132, bf16[768,768]{1,0:T(8,128)(2,1)} %bitcast.134, ...), kind=kOutput, calls=%fused_computation.10 | convolution fusion | flops 649297920 | bytes 9063424 | tf_op jit(solution)/shard_map/dot_general | solution.py:474
  119.4 2.9 slice.134
  123.3 1.2 copy-done.7
  126.0 1.5 fusion.23
  129.3 2.2 convert_reduce_fusion.5
  131.5 5.8 %convert_reduce_fusion = (bf16[3072]{0:T(1024)(128)(2,1)}, bf16[128,3072]{1,0:T(8,128)(2,1)S(1)}) fusion(f32[128,3072]{1,0:T(8,128)} %get-tuple-element.38, f32[128,3072]{1,0:T(8,128)} %get-tuple-element.72, bf16[3072,768]{1,0:T(8,128)(2,1)} %bitcast.111, f32[128,768]{1,0:T(8,128)S(1)} %get-tuple-element.34), kind=kOutput, calls=%fused_computation.8 | convolution fusion | flops 610366464 | bytes 9050112 | tf_op jit(solution)/shard_map/to,io->ti/dot_general | solution.py:360
  137.3 2.3 multiply_reduce_fusion.1
  142.3 1.7 multiply_reduce_fusion
  147.0 1.3 convolution_add_fusion.2
  148.3 1.9 convert_reduce_fusion.3
  150.2 1.3 convolution_add_fusion.1
  152.0 1.1 constant_dynamic-update-slice_fusion.8
  153.7 1.1 constant_dynamic-update-slice_fusion.7
  156.8 1.1 constant_dynamic-update-slice_fusion.5
  158.3 1.5 convolution_convert_fusion.1
  160.1 1.1 constant_dynamic-update-slice_fusion.4
  161.2 1.1 constant_dynamic-update-slice_fusion.3
  162.3 1.1 constant_dynamic-update-slice_fusion.2
  163.4 1.1 constant_dynamic-update-slice_fusion.1
  165.1 1.7 convolution_convert_fusion
  166.9 2.5 constant_dynamic-update-slice_fusion
  170.5 2.6 fusion.16.x_ref
  173.1 126.3 %sum_grads.1 = f32[304,768]{1,0:T(8,128)S(1)} custom-call(bf16[32,304,768]{2,1,0:T(8,128)(2,1)} %fusion.16.x_ref), custom_call_target="tpu_custom_call" | custom-call | tf_op jit(solution)/shard_map/sum_grads/pallas_call | solution.py:301
  (218 shorter events, 33.7 us)
Async XLA Ops:
  82.0 5.3 %copy-start = (bf16[32,304,768]{2,1,0:T(8,128)(2,1)}, bf16[32,304,768]{2,1,0:T(8,128)(2,1)S(1)}, u32[]{:S(2)}) copy-start(bf16[32,304,768]{2,1,0:T(8,128)(2,1)S(1)} %gather_params.1) | copy-start | bytes 44826628
  97.0 7.8 %copy-start.8 = (bf16[32,24,768]{2,1,0:T(8,128)(2,1)}, bf16[32,24,768]{2,1,0:T(8,128)(2,1)S(1)}, u32[]{:S(2)}) copy-start(bf16[32,24,768]{2,1,0:T(8,128)(2,1)S(1)} %get-tuple-element.44) | copy-start | bytes 3538948
  107.7 11.7 %copy-start.26 = (bf16[12,64,128]{2,1,0:T(8,128)(2,1)}, bf16[12,64,128]{2,1,0:T(8,128)(2,1)S(1)}, u32[]{:S(2)}) copy-start(bf16[12,64,128]{2,1,0:T(8,128)(2,1)S(1)} %convolution_convert_fusion.8) | copy-start | bytes 589828
  109.9 12.4 %copy-start.40 = (f32[128]{0:T(128)}, f32[128]{0:T(128)S(1)}, u32[]{:S(2)}) copy-start(f32[128]{0:T(128)S(1)} %broadcast_multiply_fusion.5) | copy-start | bytes 1540
  110.1 12.2 %copy-start.45 = (f32[128]{0:T(128)}, f32[128]{0:T(128)S(1)}, u32[]{:S(2)}) copy-start(f32[128]{0:T(128)S(1)} %add_rsqrt_fusion.1) | copy-start | bytes 1540
  119.4 3.0 copy-start.13
  119.4 3.0 copy-start.37
  122.4 3.6 %copy-start.28 = (bf16[128,768]{1,0:T(8,128)(2,1)S(1)}, bf16[128,768]{1,0:T(8,128)(2,1)}, u32[]{:S(2)}) copy-start(bf16[128,768]{1,0:T(8,128)(2,1)} %param.35) | copy-start | bytes 589828
  124.5 4.0 %copy-start.53 = (f32[128]{0:T(128)}, f32[128]{0:T(128)S(1)}, u32[]{:S(2)}) copy-start(f32[128]{0:T(128)S(1)} %broadcast_multiply_fusion.4) | copy-start | bytes 1540
  131.5 5.8 %copy-start.17 = (f32[128,768]{1,0:T(8,128)}, f32[128,768]{1,0:T(8,128)S(1)}, u32[]{:S(2)}) copy-start(f32[128,768]{1,0:T(8,128)S(1)} %get-tuple-element.34) | copy-start | bytes 1179652
  131.5 5.8 %copy-start.20 = (bf16[32,24,768]{2,1,0:T(8,128)(2,1)S(1)}, bf16[32,24,768]{2,1,0:T(8,128)(2,1)}, u32[]{:S(2)}) copy-start(bf16[32,24,768]{2,1,0:T(8,128)(2,1)} %get-tuple-element.40) | copy-start | bytes 3538948
  131.5 5.8 %copy-start.21 = (bf16[32,24,768]{2,1,0:T(8,128)(2,1)S(1)}, bf16[32,24,768]{2,1,0:T(8,128)(2,1)}, u32[]{:S(2)}) copy-start(bf16[32,24,768]{2,1,0:T(8,128)(2,1)} %get-tuple-element.41) | copy-start | bytes 3538948
  131.5 5.8 %copy-start.22 = (bf16[32,24,768]{2,1,0:T(8,128)(2,1)S(1)}, bf16[32,24,768]{2,1,0:T(8,128)(2,1)}, u32[]{:S(2)}) copy-start(bf16[32,24,768]{2,1,0:T(8,128)(2,1)} %get-tuple-element.43) | copy-start | bytes 3538948
  131.5 5.8 %copy-start.23 = (bf16[32,24,768]{2,1,0:T(8,128)(2,1)S(1)}, bf16[32,24,768]{2,1,0:T(8,128)(2,1)}, u32[]{:S(2)}) copy-start(bf16[32,24,768]{2,1,0:T(8,128)(2,1)} %get-tuple-element.45) | copy-start | bytes 3538948
  131.5 5.8 %copy-start.41 = (f32[128]{0:T(128)S(1)}, f32[128]{0:T(128)}, u32[]{:S(2)}) copy-start(f32[128]{0:T(128)} %copy-done.40) | copy-start | bytes 1540
  131.5 5.8 %copy-start.46 = (f32[128]{0:T(128)S(1)}, f32[128]{0:T(128)}, u32[]{:S(2)}) copy-start(f32[128]{0:T(128)} %copy-done.45) | copy-start | bytes 1540
  166.7 2.9 copy-start.51
  166.7 3.0 copy-start.73
  166.7 3.1 %copy-start.72 = (bf16[768]{0:T(1024)(128)(2,1)S(1)}, bf16[768]{0:T(1024)(128)(2,1)}, u32[]{:S(2)}) copy-start(bf16[768]{0:T(1024)(128)(2,1)} %get-tuple-element.30) | copy-start | bytes 4612
  166.8 3.2 %copy-start.52 = (bf16[3072]{0:T(1024)(128)(2,1)S(1)}, bf16[3072]{0:T(1024)(128)(2,1)}, u32[]{:S(2)}) copy-start(bf16[3072]{0:T(1024)(128)(2,1)} %get-tuple-element.82) | copy-start | bytes 18436
  166.8 3.3 %copy-start.50 = (bf16[768]{0:T(1024)(128)(2,1)S(1)}, bf16[768]{0:T(1024)(128)(2,1)}, u32[]{:S(2)}) copy-start(bf16[768]{0:T(1024)(128)(2,1)} %get-tuple-element.33) | copy-start | bytes 4612
  166.8 3.4 %copy-start.49 = (bf16[768]{0:T(1024)(128)(2,1)S(1)}, bf16[768]{0:T(1024)(128)(2,1)}, u32[]{:S(2)}) copy-start(bf16[768]{0:T(1024)(128)(2,1)} %get-tuple-element.27) | copy-start | bytes 4612
  166.8 3.5 %copy-start.48 = (bf16[768]{0:T(1024)(128)(2,1)S(1)}, bf16[768]{0:T(1024)(128)(2,1)}, u32[]{:S(2)}) copy-start(bf16[768]{0:T(1024)(128)(2,1)} %get-tuple-element.32) | copy-start | bytes 4612
  166.8 3.6 %copy-start.55 = (pred[16]{0:T(512)(128)(4,1)S(1)}, pred[16]{0:T(512)(128)(4,1)}, u32[]{:S(2)}) copy-start(pred[16]{0:T(512)(128)(4,1)} %copy-done.54) | copy-start | bytes 52
  166.8 3.6 %copy-start.57 = (pred[16]{0:T(512)(128)(4,1)S(1)}, pred[16]{0:T(512)(128)(4,1)}, u32[]{:S(2)}) copy-start(pred[16]{0:T(512)(128)(4,1)} %copy-done.56) | copy-start | bytes 52
  166.8 3.6 %copy-start.59 = (pred[16]{0:T(512)(128)(4,1)S(1)}, pred[16]{0:T(512)(128)(4,1)}, u32[]{:S(2)}) copy-start(pred[16]{0:T(512)(128)(4,1)} %copy-done.58) | copy-start | bytes 52
  166.8 3.6 %copy-start.61 = (pred[16]{0:T(512)(128)(4,1)S(1)}, pred[16]{0:T(512)(128)(4,1)}, u32[]{:S(2)}) copy-start(pred[16]{0:T(512)(128)(4,1)} %copy-done.60) | copy-start | bytes 52
  166.9 3.6 %copy-start.63 = (pred[16]{0:T(512)(128)(4,1)S(1)}, pred[16]{0:T(512)(128)(4,1)}, u32[]{:S(2)}) copy-start(pred[16]{0:T(512)(128)(4,1)} %copy-done.62) | copy-start | bytes 52
  166.9 3.6 %copy-start.65 = (pred[16]{0:T(512)(128)(4,1)S(1)}, pred[16]{0:T(512)(128)(4,1)}, u32[]{:S(2)}) copy-start(pred[16]{0:T(512)(128)(4,1)} %copy-done.64) | copy-start | bytes 52
  166.9 3.6 %copy-start.67 = (pred[16]{0:T(512)(128)(4,1)S(1)}, pred[16]{0:T(512)(128)(4,1)}, u32[]{:S(2)}) copy-start(pred[16]{0:T(512)(128)(4,1)} %copy-done.66) | copy-start | bytes 52
  166.9 3.6 %copy-start.69 = (pred[16]{0:T(512)(128)(4,1)S(1)}, pred[16]{0:T(512)(128)(4,1)}, u32[]{:S(2)}) copy-start(pred[16]{0:T(512)(128)(4,1)} %copy-done.68) | copy-start | bytes 52
  166.9 3.6 %copy-start.71 = (pred[16]{0:T(512)(128)(4,1)S(1)}, pred[16]{0:T(512)(128)(4,1)}, u32[]{:S(2)}) copy-start(pred[16]{0:T(512)(128)(4,1)} %copy-done.70) | copy-start | bytes 52
  (43 other events, 54.7 us)

commit v2 on v1

--- a/solution.py
+++ b/solution.py
@@ -64,6 +64,23 @@
     return slab
 
 
+def together(counts, visits):
+    least = min(counts)
+    if any(count % least for count in counts):
+        for count, visit in zip(counts, visits):
+            together([count], [visit])
+        return
+
+    def step(t, _):
+        for count, visit in zip(counts, visits):
+            times = count // least
+            for u in range(times):
+                visit(t * times + u)
+        return 0
+
+    lax.fori_loop(0, least, step, 0)
+
+
 def whoami(fsdp):
     return lax.axis_index("dp") * fsdp + lax.axis_index("fsdp")
 
@@ -121,6 +138,7 @@
         bases.append(base)
     depth = len(plan[0][2])
     for i in range(-1, depth):
+        counts, visits = [], []
         for band in range(len(plan)):
             order = plan[band][2]
             tree = order[:0:-1] + order[:1]
@@ -140,15 +158,17 @@
             dim = tree[i]
             mine = coord(me, dim)
 
-            def arrived(k, _, i=i, band=band, tree=tree, dim=dim, mine=mine, sends=sends):
+            def arrived(k, i=i, band=band, tree=tree, dim=dim, mine=mine, sends=sends):
                 gap = dim[1] - 1
                 peer = moved(me, dim, mine, lax.rem(mine + 1 + lax.rem(k, gap), dim[1]))
                 slab = spread(peer, me, tree[:i], k // gap)
                 copy_of(band, slab, 0, peer, False).wait_recv()
                 sends(slab, k, lambda c: c.start())
-                return 0
-
-            lax.fori_loop(0, prod_of(tree[:i]) * (dim[1] - 1), arrived, 0)
+
+            counts.append(prod_of(tree[:i]) * (dim[1] - 1))
+            visits.append(arrived)
+        if i >= 0:
+            together(counts, visits)
     own.wait()
     for band in range(len(plan)):
         peer = moved(me, plan[band][2][0], coord(me, plan[band][2][0]), 1 - coord(me, plan[band][2][0]))
@@ -218,34 +238,32 @@
             x_ref.at[slab, pl.ds(start, rows), :], kept[band].at[index], own_sem.at[band, index]
         )
 
-    def walk(band, i, visit):
+    def step_of(band, i, t):
         order = plan[band][2]
         if i == depth - 1:
-            visit(0, 0, 0)
-            return
+            return 0, 0, 0
         dim = order[i + 1]
         inner = prod_of(order[i + 2 :])
-        for r in range(dim[1]):
-            at = lax.rem(coord(me, dim) + 1 + r, dim[1])
-
-            def one(rest, _, r=r, at=at):
-                visit(r, rest, at * inner + rest)
-                return 0
-
-            lax.fori_loop(0, inner, one, 0)
-
+        r, rest = t // inner, lax.rem(t, inner)
+        return r, rest, lax.rem(coord(me, dim) + 1 + r, dim[1]) * inner + rest
+
+    counts, visits = [], []
     for band in range(bands):
         start, rows, order = plan[band]
         core = order[0]
         mine = coord(me, core)
 
-        def begin(r, rest, index, band=band, start=start, rows=rows, order=order, core=core, mine=mine):
+        def begin(t, band=band, start=start, rows=rows, order=order, core=core, mine=mine):
+            index = step_of(band, 0, t)[2]
             slab = moved(spread(me, me, order[1:], index), core, mine, lax.rem(mine + 1, core[1]))
             sending(band, 0, x_ref.at[slab, pl.ds(start, rows), :], 0, index).start()
             own_copy(band, index).start()
 
-        walk(band, 0, begin)
+        counts.append(prod_of(order[1:]))
+        visits.append(begin)
+    together(counts, visits)
     for i in range(depth):
+        counts, visits = [], []
         for band in range(bands):
             start, rows, order = plan[band]
             gap = order[i][1] - 1
@@ -254,7 +272,8 @@
                 where = where * dim[1] + coord(me, dim)
             where = where * prod_of(order[i + 1 :])
 
-            def visit(r, rest, index, i=i, band=band, start=start, rows=rows, order=order, gap=gap, where=where):
+            def visit(t, i=i, band=band, start=start, rows=rows, order=order, gap=gap, where=where):
+                r, rest, index = step_of(band, i, t)
                 if i == 0:
                     own_copy(band, index).wait()
                 total = kept[band][where + index].astype(f32)
@@ -273,10 +292,14 @@
                     out_ref[start : start + rows, :] = total
                     return
                 kept[band][where + index] = total.astype(kept[band].dtype)
-                if r < order[i + 1][1] - 1:
+
+                @pl.when(r < order[i + 1][1] - 1)
+                def _():
                     sending(band, i + 1, kept[band].at[where + index], r, rest).start()
 
-            walk(band, i, visit)
+            counts.append(prod_of(order[i + 1 :]))
+            visits.append(visit)
+        together(counts, visits)
     for band in range(bands):
         start, rows, order = plan[band]
 

time: 308 us -> 296 us (0.961); the launches traced: 303 us -> 295 us
  Pallas kernels: 198 us -> 191 us
    pallas_call x1, Pallas kernels: 126 us -> 120 us  [sum_shards(): pl.pallas_call(partial(sum_kernel, dp, fsdp, plan), out_shape=jax.ShapeDt...]
where the time goes in v2:
time: 296 us; the launch traced here: 295 us
  Pallas kernels  191 us (65%)
  local copies, waits for them, and re-layouts  51.2 us (17%)
  matrix products  39.8 us (13%)
  other arithmetic  11.9 us (4%)
    pallas_call x1, Pallas kernels, sum_shards(): pl.pallas_call(partial(sum_kernel, dp, fsdp, plan), out_shape=jax.ShapeDt...  120 us
    pallas_call x1, Pallas kernels, gather(): pl.pallas_call(partial(gather_kernel, dp, fsdp, plan), out_shape=jax.Shap...  70.4 us
    unnamed x159, local copies, waits for them, and re-layouts  27.4 us
    dot_general x6, matrix products, backdot(): jnp.einsum('to,io->ti', left, right, preferred_element_type=jnp.float32)  11.7 us
    dot_general x1, matrix products, on_device(): jnp.dot(first_low, params['up_weight'], preferred_element_type=f32)  9.24 us
    slice x1, local copies, waits for them, and re-layouts, matrix(): return slabs[:, k * part:(k + 1) * part, :].reshape(n * part, width)  6.42 us

profile of v2, /device:TPU:0, one launch (start us, length us, event | category | flops | bytes accessed | tf_op | source)
XLA Modules:
  0.0 295.1 jit_solution(12174295381212590335)
XLA Ops:
  10.2 70.4 %gather_params.1 = bf16[32,304,768]{2,1,0:T(8,128)(2,1)S(1)} custom-call(bf16[24,768]{1,0:T(8,128)(2,1)S(1)} %copy-done.3, bf16[24,768]{1,0:T(8,128)(2,1)S(1)} %copy-done.4, bf16[24,768]{1,0:T(8,128)(2,1)S(1)} %copy-done.5, bf16[24,768]{1,0:T(8,128)(2,1)S(1)} %copy-done.6, bf16[24,3072]{1,0:T(8,128)(2,1)S(1)} %copy-done.1, bf16[96,768]{1,0:T(8,128)(2,1)S(1)} %copy-done.2, ...), custom_call_target="tpu_custom_call" | custom-call | tf_op jit(solution)/shard_map/gather_params/pallas_call | solution.py:186
  80.7 5.3 %copy-done = bf16[32,304,768]{2,1,0:T(8,128)(2,1)} copy-done((bf16[32,304,768]{2,1,0:T(8,128)(2,1)}, bf16[32,304,768]{2,1,0:T(8,128)(2,1)S(1)}, u32[]{:S(2)}) %copy-start) | copy-done | bytes 14942232
  89.2 6.4 %fusion.43 = (bf16[32,24,768]{2,1,0:T(8,128)(2,1)}, bf16[32,24,768]{2,1,0:T(8,128)(2,1)}, bf16[32,24,768]{2,1,0:T(8,128)(2,1)}, bf16[32,24,768]{2,1,0:T(8,128)(2...) fusion(bf16[32,304,768]{2,1,0:T(8,128)(2,1)} %copy-done), kind=kLoop, calls=%fused_computation.149 | loop fusion | bytes 18874368 | tf_op jit(solution)/shard_map/slice | solution.py:441
  95.6 1.4 reshape.333
  97.0 1.4 reshape.331
  98.4 2.1 fusion.12
  101.2 2.2 fusion.13
  104.3 1.3 fusion.46
  106.6 1.7 fusion.47
  108.7 9.2 %multiply_convert_fusion = (bf16[128,3072]{1,0:T(8,128)(2,1)S(1)}, f32[128,3072]{1,0:T(8,128)}, f32[128,3072]{1,0:T(8,128)}) fusion(f32[3072]{0:T(1024)S(1)} %copy-done.42, bf16[768,768]{1,0:T(8,128)(2,1)} %bitcast.136, bf16[768,768]{1,0:T(8,128)(2,1)} %bitcast.138, bf16[768,768]{1,0:T(8,128)(2,1)} %bitcast.132, bf16[768,768]{1,0:T(8,128)(2,1)} %bitcast.134, ...), kind=kOutput, calls=%fused_computation.10 | convolution fusion | flops 649297920 | bytes 9063424 | tf_op jit(solution)/shard_map/dot_general | solution.py:497
  118.0 2.9 slice.134
  121.9 1.2 copy-done.7
  124.6 1.5 fusion.23
  127.9 2.2 convert_reduce_fusion.5
  130.1 5.8 %convert_reduce_fusion = (bf16[3072]{0:T(1024)(128)(2,1)}, bf16[128,3072]{1,0:T(8,128)(2,1)S(1)}) fusion(f32[128,3072]{1,0:T(8,128)} %get-tuple-element.38, f32[128,3072]{1,0:T(8,128)} %get-tuple-element.72, bf16[3072,768]{1,0:T(8,128)(2,1)} %bitcast.111, f32[128,768]{1,0:T(8,128)S(1)} %get-tuple-element.34), kind=kOutput, calls=%fused_computation.8 | convolution fusion | flops 610366464 | bytes 9050112 | tf_op jit(solution)/shard_map/to,io->ti/dot_general | solution.py:383
  135.9 2.3 multiply_reduce_fusion.1
  140.9 1.7 multiply_reduce_fusion
  145.6 1.3 convolution_add_fusion.2
  146.9 1.9 convert_reduce_fusion.3
  148.8 1.3 convolution_add_fusion.1
  150.6 1.1 constant_dynamic-update-slice_fusion.8
  152.3 1.1 constant_dynamic-update-slice_fusion.7
  155.4 1.1 constant_dynamic-update-slice_fusion.5
  156.9 1.5 convolution_convert_fusion.1
  158.7 1.1 constant_dynamic-update-slice_fusion.4
  159.8 1.1 constant_dynamic-update-slice_fusion.3
  160.9 1.1 constant_dynamic-update-slice_fusion.2
  162.0 1.1 constant_dynamic-update-slice_fusion.1
  163.6 1.7 convolution_convert_fusion
  165.5 2.5 constant_dynamic-update-slice_fusion
  169.1 2.6 fusion.16.x_ref
  171.7 120.1 %sum_grads.1 = f32[304,768]{1,0:T(8,128)S(1)} custom-call(bf16[32,304,768]{2,1,0:T(8,128)(2,1)} %fusion.16.x_ref), custom_call_target="tpu_custom_call" | custom-call | tf_op jit(solution)/shard_map/sum_grads/pallas_call | solution.py:324
  (218 shorter events, 33.7 us)
Async XLA Ops:
  80.6 5.3 %copy-start = (bf16[32,304,768]{2,1,0:T(8,128)(2,1)}, bf16[32,304,768]{2,1,0:T(8,128)(2,1)S(1)}, u32[]{:S(2)}) copy-start(bf16[32,304,768]{2,1,0:T(8,128)(2,1)S(1)} %gather_params.1) | copy-start | bytes 44826628
  95.6 7.8 %copy-start.8 = (bf16[32,24,768]{2,1,0:T(8,128)(2,1)}, bf16[32,24,768]{2,1,0:T(8,128)(2,1)S(1)}, u32[]{:S(2)}) copy-start(bf16[32,24,768]{2,1,0:T(8,128)(2,1)S(1)} %get-tuple-element.44) | copy-start | bytes 3538948
  106.3 11.7 %copy-start.26 = (bf16[12,64,128]{2,1,0:T(8,128)(2,1)}, bf16[12,64,128]{2,1,0:T(8,128)(2,1)S(1)}, u32[]{:S(2)}) copy-start(bf16[12,64,128]{2,1,0:T(8,128)(2,1)S(1)} %convolution_convert_fusion.8) | copy-start | bytes 589828
  108.5 12.4 %copy-start.40 = (f32[128]{0:T(128)}, f32[128]{0:T(128)S(1)}, u32[]{:S(2)}) copy-start(f32[128]{0:T(128)S(1)} %broadcast_multiply_fusion.5) | copy-start | bytes 1540
  108.7 12.2 %copy-start.45 = (f32[128]{0:T(128)}, f32[128]{0:T(128)S(1)}, u32[]{:S(2)}) copy-start(f32[128]{0:T(128)S(1)} %add_rsqrt_fusion.1) | copy-start | bytes 1540
  118.0 3.0 %copy-start.13 = (bf16[128,3072]{1,0:T(8,128)(2,1)}, bf16[128,3072]{1,0:T(8,128)(2,1)S(1)}, u32[]{:S(2)}) copy-start(bf16[128,3072]{1,0:T(8,128)(2,1)S(1)} %get-tuple-element.37) | copy-start | bytes 2359300
  118.0 3.0 %copy-start.37 = (f32[768]{0:T(1024)S(1)}, f32[768]{0:T(1024)}, u32[]{:S(2)}) copy-start(f32[768]{0:T(1024)} %reshape.337) | copy-start | bytes 9220
  121.0 3.6 %copy-start.28 = (bf16[128,768]{1,0:T(8,128)(2,1)S(1)}, bf16[128,768]{1,0:T(8,128)(2,1)}, u32[]{:S(2)}) copy-start(bf16[128,768]{1,0:T(8,128)(2,1)} %param.35) | copy-start | bytes 589828
  123.1 4.0 %copy-start.53 = (f32[128]{0:T(128)}, f32[128]{0:T(128)S(1)}, u32[]{:S(2)}) copy-start(f32[128]{0:T(128)S(1)} %broadcast_multiply_fusion.4) | copy-start | bytes 1540
  130.1 5.8 %copy-start.17 = (f32[128,768]{1,0:T(8,128)}, f32[128,768]{1,0:T(8,128)S(1)}, u32[]{:S(2)}) copy-start(f32[128,768]{1,0:T(8,128)S(1)} %get-tuple-element.34) | copy-start | bytes 1179652
  130.1 5.8 %copy-start.20 = (bf16[32,24,768]{2,1,0:T(8,128)(2,1)S(1)}, bf16[32,24,768]{2,1,0:T(8,128)(2,1)}, u32[]{:S(2)}) copy-start(bf16[32,24,768]{2,1,0:T(8,128)(2,1)} %get-tuple-element.40) | copy-start | bytes 3538948
  130.1 5.8 %copy-start.21 = (bf16[32,24,768]{2,1,0:T(8,128)(2,1)S(1)}, bf16[32,24,768]{2,1,0:T(8,128)(2,1)}, u32[]{:S(2)}) copy-start(bf16[32,24,768]{2,1,0:T(8,128)(2,1)} %get-tuple-element.41) | copy-start | bytes 3538948
  130.1 5.8 %copy-start.22 = (bf16[32,24,768]{2,1,0:T(8,128)(2,1)S(1)}, bf16[32,24,768]{2,1,0:T(8,128)(2,1)}, u32[]{:S(2)}) copy-start(bf16[32,24,768]{2,1,0:T(8,128)(2,1)} %get-tuple-element.43) | copy-start | bytes 3538948
  130.1 5.8 %copy-start.23 = (bf16[32,24,768]{2,1,0:T(8,128)(2,1)S(1)}, bf16[32,24,768]{2,1,0:T(8,128)(2,1)}, u32[]{:S(2)}) copy-start(bf16[32,24,768]{2,1,0:T(8,128)(2,1)} %get-tuple-element.45) | copy-start | bytes 3538948
  130.1 5.8 %copy-start.41 = (f32[128]{0:T(128)S(1)}, f32[128]{0:T(128)}, u32[]{:S(2)}) copy-start(f32[128]{0:T(128)} %copy-done.40) | copy-start | bytes 1540
  130.1 5.8 %copy-start.46 = (f32[128]{0:T(128)S(1)}, f32[128]{0:T(128)}, u32[]{:S(2)}) copy-start(f32[128]{0:T(128)} %copy-done.45) | copy-start | bytes 1540
  165.3 2.9 copy-start.51
  165.3 3.0 %copy-start.73 = (bf16[768]{0:T(1024)(128)(2,1)S(1)}, bf16[768]{0:T(1024)(128)(2,1)}, u32[]{:S(2)}) copy-start(bf16[768]{0:T(1024)(128)(2,1)} %get-tuple-element.25) | copy-start | bytes 4612
  165.3 3.1 %copy-start.72 = (bf16[768]{0:T(1024)(128)(2,1)S(1)}, bf16[768]{0:T(1024)(128)(2,1)}, u32[]{:S(2)}) copy-start(bf16[768]{0:T(1024)(128)(2,1)} %get-tuple-element.30) | copy-start | bytes 4612
  165.4 3.2 %copy-start.52 = (bf16[3072]{0:T(1024)(128)(2,1)S(1)}, bf16[3072]{0:T(1024)(128)(2,1)}, u32[]{:S(2)}) copy-start(bf16[3072]{0:T(1024)(128)(2,1)} %get-tuple-element.82) | copy-start | bytes 18436
  165.4 3.3 %copy-start.50 = (bf16[768]{0:T(1024)(128)(2,1)S(1)}, bf16[768]{0:T(1024)(128)(2,1)}, u32[]{:S(2)}) copy-start(bf16[768]{0:T(1024)(128)(2,1)} %get-tuple-element.33) | copy-start | bytes 4612
  165.4 3.4 %copy-start.49 = (bf16[768]{0:T(1024)(128)(2,1)S(1)}, bf16[768]{0:T(1024)(128)(2,1)}, u32[]{:S(2)}) copy-start(bf16[768]{0:T(1024)(128)(2,1)} %get-tuple-element.27) | copy-start | bytes 4612
  165.4 3.5 %copy-start.48 = (bf16[768]{0:T(1024)(128)(2,1)S(1)}, bf16[768]{0:T(1024)(128)(2,1)}, u32[]{:S(2)}) copy-start(bf16[768]{0:T(1024)(128)(2,1)} %get-tuple-element.32) | copy-start | bytes 4612
  165.4 3.6 %copy-start.55 = (pred[16]{0:T(512)(128)(4,1)S(1)}, pred[16]{0:T(512)(128)(4,1)}, u32[]{:S(2)}) copy-start(pred[16]{0:T(512)(128)(4,1)} %copy-done.54) | copy-start | bytes 52
  165.4 3.6 %copy-start.57 = (pred[16]{0:T(512)(128)(4,1)S(1)}, pred[16]{0:T(512)(128)(4,1)}, u32[]{:S(2)}) copy-start(pred[16]{0:T(512)(128)(4,1)} %copy-done.56) | copy-start | bytes 52
  165.4 3.6 %copy-start.59 = (pred[16]{0:T(512)(128)(4,1)S(1)}, pred[16]{0:T(512)(128)(4,1)}, u32[]{:S(2)}) copy-start(pred[16]{0:T(512)(128)(4,1)} %copy-done.58) | copy-start | bytes 52
  165.4 3.6 %copy-start.61 = (pred[16]{0:T(512)(128)(4,1)S(1)}, pred[16]{0:T(512)(128)(4,1)}, u32[]{:S(2)}) copy-start(pred[16]{0:T(512)(128)(4,1)} %copy-done.60) | copy-start | bytes 52
  165.4 3.6 %copy-start.63 = (pred[16]{0:T(512)(128)(4,1)S(1)}, pred[16]{0:T(512)(128)(4,1)}, u32[]{:S(2)}) copy-start(pred[16]{0:T(512)(128)(4,1)} %copy-done.62) | copy-start | bytes 52
  165.5 3.6 %copy-start.65 = (pred[16]{0:T(512)(128)(4,1)S(1)}, pred[16]{0:T(512)(128)(4,1)}, u32[]{:S(2)}) copy-start(pred[16]{0:T(512)(128)(4,1)} %copy-done.64) | copy-start | bytes 52
  165.5 3.6 %copy-start.67 = (pred[16]{0:T(512)(128)(4,1)S(1)}, pred[16]{0:T(512)(128)(4,1)}, u32[]{:S(2)}) copy-start(pred[16]{0:T(512)(128)(4,1)} %copy-done.66) | copy-start | bytes 52
  165.5 3.6 %copy-start.69 = (pred[16]{0:T(512)(128)(4,1)S(1)}, pred[16]{0:T(512)(128)(4,1)}, u32[]{:S(2)}) copy-start(pred[16]{0:T(512)(128)(4,1)} %copy-done.68) | copy-start | bytes 52
  165.5 3.6 %copy-start.71 = (pred[16]{0:T(512)(128)(4,1)S(1)}, pred[16]{0:T(512)(128)(4,1)}, u32[]{:S(2)}) copy-start(pred[16]{0:T(512)(128)(4,1)} %copy-done.70) | copy-start | bytes 52
  (43 other events, 54.7 us)

commit v3 on v2

--- a/solution.py
+++ b/solution.py
@@ -1,3 +1,4 @@
+import math
 from functools import partial
 
 import jax
@@ -358,6 +359,44 @@
     "second_shift",
 ]
 VECTORS = [name for name in PARAM_NAMES if not name.endswith("_weight")]
+
+def terms_kernel(part, tall, *refs):
+    tokens, d_query, d_keys, d_values, attended, d_branch, first_low, d_hidden, active, d_down, flat, out_ref = refs
+    width = out_ref.shape[2]
+
+    def product(left, right, start, count, rows):
+        whole = lax.dot_general(
+            left[:, start : start + count], right, (((0,), (0,)), ((), ())), preferred_element_type=jnp.float32
+        )
+        return whole.reshape(count // rows, rows, width)
+
+    pairs = [(tokens, d_query[...]), (tokens, d_keys[...]), (tokens, d_values[...]), (attended, d_branch[...])]
+    for j in range(d_hidden.shape[1] // width):
+        pairs.append((first_low, d_hidden[:, j * width : (j + 1) * width]))
+    count = math.lcm(part, 128)
+    for start in range(0, width, count):
+        slabs = slice(start // part, (start + count) // part)
+        for k in range(0, len(pairs), 2):
+            two = [product(left, right, start, count, part) for left, right in pairs[k : k + 2]]
+            out_ref[slabs, k * part : (k + 2) * part, :] = jnp.concatenate(two, axis=1).astype(out_ref.dtype)
+    count, at = math.lcm(tall, 128), len(pairs) * part
+    for start in range(0, active.shape[1], count):
+        slabs = slice(start // tall, (start + count) // tall)
+        out_ref[slabs, at : at + tall, :] = product(active, d_down[...], start, count, tall).astype(out_ref.dtype)
+    out_ref[:, at + tall :, :] = flat[...]
+
+
+def terms_by_owner(part, tall, rows, operands):
+    n, _, width = operands[-1].shape
+    return pl.pallas_call(
+        partial(terms_kernel, part, tall),
+        out_shape=jax.ShapeDtypeStruct((n, rows, width), jnp.bfloat16),
+        in_specs=[pl.BlockSpec(memory_space=pltpu.VMEM)] * len(operands),
+        out_specs=pl.BlockSpec(memory_space=pltpu.VMEM),
+        compiler_params=pltpu.CompilerParams(vmem_limit_bytes=32 * 1024 * 1024),
+        name="terms_by_owner",
+    )(*operands)
+
 
 def normalize(rows, gain, shift):
     centred = rows - jnp.mean(rows, axis=-1, keepdims=True)
@@ -516,17 +555,14 @@
     d_second = norm_back(grad_out, normed_second, scale_second, gain_second)
     d_down = d_second.astype(bf16)
     grads["down_bias"] = jnp.sum(d_down.astype(f32), axis=0)
-    grads["down_weight"] = rowdot(active, d_down)
     d_hidden = gelu_back(backdot(d_down, params["down_weight"]))[0].astype(bf16)
     grads["up_bias"] = jnp.sum(d_hidden.astype(f32), axis=0)
-    grads["up_weight"] = rowdot(first_low, d_hidden)
     d_first = d_second + backdot(d_hidden, params["up_weight"])
     grads["first_gain"] = jnp.sum(d_first * normed_first, axis=0)
     grads["first_shift"] = jnp.sum(d_first, axis=0)
     d_branch_full = norm_back(d_first, normed_first, scale_first, gain_first)
     d_branch = d_branch_full.astype(bf16)
     grads["out_bias"] = jnp.sum(d_branch.astype(f32), axis=0)
-    grads["out_weight"] = rowdot(attended, d_branch)
     d_attended = split_heads(backdot(d_branch, params["out_weight"]).astype(bf16))
     d_probs = jnp.einsum(
         "qhd,khd->hqk", d_attended, split_heads(values), preferred_element_type=f32
@@ -553,9 +589,6 @@
         .reshape(length, width)
         .astype(bf16)
     )
-    grads["query_weight"] = rowdot(tokens, d_query)
-    grads["key_weight"] = rowdot(tokens, d_keys)
-    grads["value_weight"] = rowdot(tokens, d_values)
     grads["query_bias"] = jnp.sum(d_query.astype(f32), axis=0)
     grads["value_bias"] = jnp.sum(d_values.astype(f32), axis=0)
     input_grad = (
@@ -574,13 +607,19 @@
         mine = jnp.pad(mine, ((0, 0), (0, width - mine.shape[1])))
         flat = jnp.where(row == k, mine[:, None, :], flat)
     flat = flat.astype(bf16)
-    up = grads["up_weight"].astype(bf16)
-    terms = jnp.concatenate(
-        [by_owner(grads[name + "_weight"]) for name in ("query", "key", "value", "out")]
-        + [by_owner(up[:, j * width : (j + 1) * width]) for j in range(wide)]
-        + [by_owner(grads["down_weight"]), flat],
-        axis=1,
-    )
+    operands = (tokens, d_query, d_keys, d_values, attended, d_branch, first_low, d_hidden, active, d_down, flat)
+    even = part % 8 == 0 and tall % 16 == 0 and wide % 2 == 0
+    if even and width % math.lcm(part, 128) == 0 and up_weight.shape[1] % math.lcm(tall, 128) == 0:
+        terms = terms_by_owner(part, tall, total_rows, operands)
+    else:
+        up = rowdot(first_low, d_hidden)
+        terms = jnp.concatenate(
+            [by_owner(rowdot(tokens, grad)) for grad in (d_query, d_keys, d_values)]
+            + [by_owner(rowdot(attended, d_branch))]
+            + [by_owner(up[:, j * width : (j + 1) * width]) for j in range(wide)]
+            + [by_owner(rowdot(active, d_down)), flat],
+            axis=1,
+        )
     sums = sum_shards(dp, fsdp, terms)
     owned = {}
     for k, name in enumerate(("query", "key", "value", "out")):

time: 296 us -> 277 us (0.936)
  local copies, waits for them, and re-layouts: 51.2 us -> 38.4 us
  matrix products: 39.8 us -> 27.4 us
  Pallas kernels: 191 us -> 199 us
    unnamed x159 -> x130, local copies, waits for them, and re-layouts: 27.4 us -> 13.6 us
    dot_general x6 -> x0, matrix products: 5.13 us -> none  [rowdot(): jnp.einsum('ti,to->io', left, right, preferred_element_type=jnp.float32)]
    pad x9, local copies, waits for them, and re-layouts: 0.08 us -> 5.02 us  [on_device(): mine = jnp.pad(mine, ((0, 0), (0, width - mine.shape[1])))]
    pallas_call x1, Pallas kernels: 120 us -> 125 us  [sum_shards(): pl.pallas_call(partial(sum_kernel, dp, fsdp, plan), out_shape=jax.ShapeDt...]
    pallas_call x0 -> x1, Pallas kernels: none -> 4.12 us  [terms_by_owner(): pl.pallas_call(partial(terms_kernel, part, tall), out_shape=jax.ShapeDtyp...]
where the time goes in v3:
time: 277 us; the launch traced here: 276 us
  Pallas kernels  199 us (72%)
  local copies, waits for them, and re-layouts  38.4 us (14%)
  matrix products  27.4 us (10%)
  other arithmetic  9.22 us (3%)
    pallas_call x1, Pallas kernels, sum_shards(): pl.pallas_call(partial(sum_kernel, dp, fsdp, plan), out_shape=jax.ShapeDt...  125 us
    pallas_call x1, Pallas kernels, gather(): pl.pallas_call(partial(gather_kernel, dp, fsdp, plan), out_shape=jax.Shap...  70.4 us
    unnamed x130, local copies, waits for them, and re-layouts  13.6 us
    dot_general x6, matrix products, backdot(): jnp.einsum('to,io->ti', left, right, preferred_element_type=jnp.float32)  11 us
    dot_general x1, matrix products, on_device(): jnp.dot(first_low, params['up_weight'], preferred_element_type=f32)  7.52 us
    slice x1, local copies, waits for them, and re-layouts, matrix(): return slabs[:, k * part:(k + 1) * part, :].reshape(n * part, width)  6.17 us

profile of v3, /device:TPU:0, one launch (start us, length us, event | category | flops | bytes accessed | tf_op | source)
XLA Modules:
  0.0 276.0 jit_solution(18279298367907379657)
XLA Ops:
  2.1 0.7 pad_convert_fusion.2
  2.8 0.7 pad_convert_fusion.4
  4.4 0.8 broadcast_compare_fusion
  5.2 0.9 copy-done.2
  6.1 0.9 copy-done.3
  7.0 0.8 copy-done.4
  7.8 0.8 copy-done.5
  8.5 0.8 copy-done.6
  9.3 0.8 copy-done.7
  10.1 70.4 %gather_params.1 = bf16[32,304,768]{2,1,0:T(8,128)(2,1)S(1)} custom-call(bf16[24,768]{1,0:T(8,128)(2,1)S(1)} %copy-done.4, bf16[24,768]{1,0:T(8,128)(2,1)S(1)} %copy-done.5, bf16[24,768]{1,0:T(8,128)(2,1)S(1)} %copy-done.6, bf16[24,768]{1,0:T(8,128)(2,1)S(1)} %copy-done.7, bf16[24,3072]{1,0:T(8,128)(2,1)S(1)} %copy-done.2, bf16[96,768]{1,0:T(8,128)(2,1)S(1)} %copy-done.3, ...), custom_call_target="tpu_custom_call" | custom-call | tf_op jit(solution)/shard_map/gather_params/pallas_call | solution.py:187
  80.5 5.3 %copy-done = bf16[32,304,768]{2,1,0:T(8,128)(2,1)} copy-done((bf16[32,304,768]{2,1,0:T(8,128)(2,1)}, bf16[32,304,768]{2,1,0:T(8,128)(2,1)S(1)}, u32[]{:S(2)}) %copy-start) | copy-done | bytes 14942232
  85.9 1.6 convert_reduce_fusion.7
  88.2 4.8 %slice.122 = bf16[32,96,768]{2,1,0:T(8,128)(2,1)} slice(bf16[32,304,768]{2,1,0:T(8,128)(2,1)} %copy-done), slice={[0:32], [192:288], [0:768]} | slice | bytes 9437184 | tf_op jit(solution)/shard_map/slice | solution.py:488
  93.0 6.2 %fusion.34 = (bf16[32,24,768]{2,1,0:T(8,128)(2,1)}, bf16[32,24,768]{2,1,0:T(8,128)(2,1)}, bf16[32,24,768]{2,1,0:T(8,128)(2,1)S(1)}, bf16[32,24,768]{2,1,0:T(8,12...) fusion(bf16[32,304,768]{2,1,0:T(8,128)(2,1)} %copy-done), kind=kLoop, calls=%fused_computation.129 | loop fusion | bytes 18874368 | tf_op jit(solution)/shard_map/slice | solution.py:480
  101.2 1.4 fusion.36
  105.0 7.5 %multiply_convert_fusion = (bf16[128,3072]{1,0:T(8,128)(2,1)S(1)}, f32[128,3072]{1,0:T(8,128)}, f32[128,3072]{1,0:T(8,128)}) fusion(f32[3072]{0:T(1024)S(1)} %reshape.300, bf16[128,768]{1,0:T(8,128)(2,1)S(1)} %fusion.23.refs_6_, bf16[768,768]{1,0:T(8,128)(2,1)} %bitcast.108, bf16[768,768]{1,0:T(8,128)(2,1)} %bitcast.110, bf16[768,768]{1,0:T(8,128)(2,1)S(1)} %bitcast.106, ...), kind=kOutput, calls=%fused_computation.8 | convolution fusion | flops 648806400 | bytes 8859648 | tf_op jit(solution)/shard_map/dot_general | solution.py:536
  112.5 0.9 fusion.38
  115.4 1.5 convert_reduce_fusion.5
  117.0 5.7 %convert_reduce_fusion = (bf16[3072]{0:T(1024)(128)(2,1)}, bf16[128,3072]{1,0:T(8,128)(2,1)S(1)}) fusion(f32[128,3072]{1,0:T(8,128)} %get-tuple-element.41, f32[128,3072]{1,0:T(8,128)} %get-tuple-element.71, bf16[128,768]{1,0:T(8,128)(2,1)S(1)} %get-tuple-element.34.refs_9_, bf16[3072,768]{1,0:T(8,128)(2,1)} %bitcast.88), kind=kOutput, calls=%fused_computation.6 | convolution fusion | flops 610268160 | bytes 8853504 | tf_op jit(solution)/shard_map/to,io->ti/dot_general | solution.py:422
  122.8 2.4 multiply_reduce_fusion.1
  125.2 0.9 convert_reduce_fusion.4
  127.1 0.8 copy.46
  131.6 1.7 convert_reduce_fusion.3
  134.2 1.6 multiply_reduce_fusion
  138.7 0.7 copy-done.9
  139.4 1.3 convolution_add_fusion.1
  141.2 2.6 select_convert_fusion.refs_10_
  143.8 4.1 %terms_by_owner.1.x_ref = bf16[32,304,768]{2,1,0:T(8,128)(2,1)S(1)} custom-call(bf16[128,768]{1,0:T(8,128)(2,1)S(1)} %copy-done.1, bf16[128,768]{1,0:T(8,128)(2,1)S(1)} %copy.50.refs_1_, bf16[128,768]{1,0:T(8,128)(2,1)S(1)} %copy.51.refs_2_, bf16[128,768]{1,0:T(8,128)(2,1)S(1)} %copy.52.refs_3_, bf16[128,768]{1,0:T(8,128)(2,1)S(1)} %copy.53.refs_4_, ...), custom_call_target="tpu_custom_call" | custom-call | tf_op jit(solution)/shard_map/terms_by_owner/pallas_call | solution.py:391
  147.9 124.8 %sum_grads.1 = f32[304,768]{1,0:T(8,128)S(1)} custom-call(bf16[32,304,768]{2,1,0:T(8,128)(2,1)S(1)} %terms_by_owner.1.x_ref), custom_call_target="tpu_custom_call" | custom-call | tf_op jit(solution)/shard_map/sum_grads/pallas_call | solution.py:325
  273.8 0.7 slice.140
  274.5 0.7 fusion.35
  275.3 0.7 pad_maximum_fusion.3
  (189 shorter events, 18.9 us)
Async XLA Ops:
  0.7 3.6 %copy-start.43 = (pred[16]{0:T(512)(128)(4,1)}, pred[16]{0:T(512)(128)(4,1)S(1)}, u32[]{:S(2)}) copy-start(pred[16]{0:T(512)(128)(4,1)S(1)} %iota_compare_fusion.8) | copy-start | bytes 52
  0.7 3.6 %copy-start.45 = (pred[16]{0:T(512)(128)(4,1)}, pred[16]{0:T(512)(128)(4,1)S(1)}, u32[]{:S(2)}) copy-start(pred[16]{0:T(512)(128)(4,1)S(1)} %get-tuple-element.95) | copy-start | bytes 52
  0.7 3.6 %copy-start.47 = (pred[16]{0:T(512)(128)(4,1)}, pred[16]{0:T(512)(128)(4,1)S(1)}, u32[]{:S(2)}) copy-start(pred[16]{0:T(512)(128)(4,1)S(1)} %get-tuple-element.96) | copy-start | bytes 52
  0.7 3.6 %copy-start.49 = (pred[16]{0:T(512)(128)(4,1)}, pred[16]{0:T(512)(128)(4,1)S(1)}, u32[]{:S(2)}) copy-start(pred[16]{0:T(512)(128)(4,1)S(1)} %get-tuple-element.93) | copy-start | bytes 52
  0.7 3.6 %copy-start.50 = (pred[16]{0:T(512)(128)(4,1)}, pred[16]{0:T(512)(128)(4,1)S(1)}, u32[]{:S(2)}) copy-start(pred[16]{0:T(512)(128)(4,1)S(1)} %get-tuple-element.94) | copy-start | bytes 52
  0.8 3.6 %copy-start.51 = (pred[16]{0:T(512)(128)(4,1)}, pred[16]{0:T(512)(128)(4,1)S(1)}, u32[]{:S(2)}) copy-start(pred[16]{0:T(512)(128)(4,1)S(1)} %get-tuple-element.91) | copy-start | bytes 52
  0.8 3.6 %copy-start.52 = (pred[16]{0:T(512)(128)(4,1)}, pred[16]{0:T(512)(128)(4,1)S(1)}, u32[]{:S(2)}) copy-start(pred[16]{0:T(512)(128)(4,1)S(1)} %get-tuple-element.92) | copy-start | bytes 52
  0.8 3.6 %copy-start.53 = (pred[16]{0:T(512)(128)(4,1)}, pred[16]{0:T(512)(128)(4,1)S(1)}, u32[]{:S(2)}) copy-start(pred[16]{0:T(512)(128)(4,1)S(1)} %get-tuple-element.89) | copy-start | bytes 52
  0.8 3.6 %copy-start.54 = (pred[16]{0:T(512)(128)(4,1)}, pred[16]{0:T(512)(128)(4,1)S(1)}, u32[]{:S(2)}) copy-start(pred[16]{0:T(512)(128)(4,1)S(1)} %get-tuple-element.90) | copy-start | bytes 52
  10.1 92.5 %copy-start.34 = (pred[128,128]{0,1:T(8,128)(4,1)}, pred[128,128]{0,1:T(8,128)(4,1)S(1)}, u32[]{:S(2)}) copy-start(pred[128,128]{0,1:T(8,128)(4,1)S(1)} %broadcast_compare_fusion) | copy-start | bytes 49156
  80.5 5.3 %copy-start = (bf16[32,304,768]{2,1,0:T(8,128)(2,1)}, bf16[32,304,768]{2,1,0:T(8,128)(2,1)S(1)}, u32[]{:S(2)}) copy-start(bf16[32,304,768]{2,1,0:T(8,128)(2,1)S(1)} %gather_params.1) | copy-start | bytes 44826628
  93.0 6.2 %copy-start.1 = (bf16[128,768]{1,0:T(8,128)(2,1)S(1)}, bf16[128,768]{1,0:T(8,128)(2,1)}, u32[]{:S(2)}) copy-start(bf16[128,768]{1,0:T(8,128)(2,1)} %refs_0_.3) | copy-start | bytes 589828
  99.2 4.1 %copy-start.14 = (bf16[32,24,768]{2,1,0:T(8,128)(2,1)}, bf16[32,24,768]{2,1,0:T(8,128)(2,1)S(1)}, u32[]{:S(2)}) copy-start(bf16[32,24,768]{2,1,0:T(8,128)(2,1)S(1)} %get-tuple-element.44) | copy-start | bytes 3538948
  103.8 8.7 %copy-start.35 = (f32[128]{0:T(128)}, f32[128]{0:T(128)S(1)}, u32[]{:S(2)}) copy-start(f32[128]{0:T(128)S(1)} %broadcast_multiply_fusion.5) | copy-start | bytes 1540
  103.8 8.7 %slice-start = ((s8[4718592]{0:T(1024)(128)(4,1)}), s8[4194304]{0:T(1024)(128)(4,1)S(1)}, s32[]{:S(2)}) async-start(s8[4718592]{0:T(1024)(128)(4,1)} %bitcast.89), calls=%async_computation | async-start | bytes 8388608
  104.0 8.5 %copy-start.39 = (f32[128]{0:T(128)}, f32[128]{0:T(128)S(1)}, u32[]{:S(2)}) copy-start(f32[128]{0:T(128)S(1)} %add_rsqrt_fusion.1) | copy-start | bytes 1540
  104.9 7.5 %slice-start.1 = ((s8[4718592]{0:T(1024)(128)(4,1)}), s8[524288]{0:T(1024)(128)(4,1)S(1)}, s32[]{:S(2)}) async-start(s8[4718592]{0:T(1024)(128)(4,1)} %bitcast.89), calls=%async_computation.1 | async-start | bytes 1048576
  113.4 3.4 %copy-start.41 = (f32[128]{0:T(128)}, f32[128]{0:T(128)S(1)}, u32[]{:S(2)}) copy-start(f32[128]{0:T(128)S(1)} %broadcast_multiply_fusion.4) | copy-start | bytes 1540
  113.6 3.2 %copy-start.55 = (f32[128]{0:T(128)}, f32[128]{0:T(128)S(1)}, u32[]{:S(2)}) copy-start(f32[128]{0:T(128)S(1)} %add_rsqrt_fusion) | copy-start | bytes 1540
  116.9 5.9 %copy-start.18 = (bf16[32,24,768]{2,1,0:T(8,128)(2,1)S(1)}, bf16[32,24,768]{2,1,0:T(8,128)(2,1)}, u32[]{:S(2)}) copy-start(bf16[32,24,768]{2,1,0:T(8,128)(2,1)} %get-tuple-element.42) | copy-start | bytes 3538948
  116.9 5.9 %copy-start.20 = (bf16[32,24,768]{2,1,0:T(8,128)(2,1)S(1)}, bf16[32,24,768]{2,1,0:T(8,128)(2,1)}, u32[]{:S(2)}) copy-start(bf16[32,24,768]{2,1,0:T(8,128)(2,1)} %get-tuple-element.43) | copy-start | bytes 3538948
  116.9 5.8 %copy-start.21 = (bf16[32,24,768]{2,1,0:T(8,128)(2,1)S(1)}, bf16[32,24,768]{2,1,0:T(8,128)(2,1)}, u32[]{:S(2)}) copy-start(bf16[32,24,768]{2,1,0:T(8,128)(2,1)} %get-tuple-element.46) | copy-start | bytes 3538948
  116.9 5.8 %copy-start.22 = (bf16[32,24,768]{2,1,0:T(8,128)(2,1)S(1)}, bf16[32,24,768]{2,1,0:T(8,128)(2,1)}, u32[]{:S(2)}) copy-start(bf16[32,24,768]{2,1,0:T(8,128)(2,1)} %get-tuple-element.48) | copy-start | bytes 3538948
  116.9 5.8 %copy-start.36 = (f32[128]{0:T(128)S(1)}, f32[128]{0:T(128)}, u32[]{:S(2)}) copy-start(f32[128]{0:T(128)} %copy-done.35) | copy-start | bytes 1540
  116.9 5.8 %copy-start.40 = (f32[128]{0:T(128)S(1)}, f32[128]{0:T(128)}, u32[]{:S(2)}) copy-start(f32[128]{0:T(128)} %copy-done.39) | copy-start | bytes 1540
  116.9 5.8 %copy-start.42 = (f32[128]{0:T(128)S(1)}, f32[128]{0:T(128)}, u32[]{:S(2)}) copy-start(f32[128]{0:T(128)} %copy-done.41) | copy-start | bytes 1540
  116.9 5.8 %copy-start.56 = (f32[128]{0:T(128)S(1)}, f32[128]{0:T(128)}, u32[]{:S(2)}) copy-start(f32[128]{0:T(128)} %copy-done.55) | copy-start | bytes 1540
  116.9 5.8 %copy-start.60 = (f32[128]{0:T(128)S(1)}, f32[128]{0:T(128)}, u32[]{:S(2)}) copy-start(f32[128]{0:T(128)} %copy-done.59) | copy-start | bytes 1540
  117.0 5.8 %copy-start.62 = (f32[128]{0:T(128)S(1)}, f32[128]{0:T(128)}, u32[]{:S(2)}) copy-start(f32[128]{0:T(128)} %copy-done.61) | copy-start | bytes 1540
  125.2 3.0 %copy-start.58 = (bf16[768]{0:T(1024)(128)(2,1)S(1)}, bf16[768]{0:T(1024)(128)(2,1)}, u32[]{:S(2)}) copy-start(bf16[768]{0:T(1024)(128)(2,1)} %get-tuple-element.25) | copy-start | bytes 4612
  125.2 3.1 %copy-start.57 = (bf16[768]{0:T(1024)(128)(2,1)S(1)}, bf16[768]{0:T(1024)(128)(2,1)}, u32[]{:S(2)}) copy-start(bf16[768]{0:T(1024)(128)(2,1)} %get-tuple-element.30) | copy-start | bytes 4612
  125.2 6.4 %copy-start.24 = (bf16[768,128]{1,0:T(8,128)(2,1)S(1)}, bf16[768,128]{1,0:T(8,128)(2,1)}, u32[]{:S(2)}) copy-start(bf16[768,128]{1,0:T(8,128)(2,1)} %copy-done.23) | copy-start | bytes 589828
  (33 other events, 53.5 us)
